TPU v7x, 256 devices: a whole 4x4x8 slice. The times are simulated.
256 devices in a mesh: seq: 16 (over y, z_hi, core), dp: 16 (over x, z_lo).
Axes of the slice: x: 4, y: 4, z: 8 (z_hi: 2, z_lo: 4; z = z_hi * 4 + z_lo), core: 2. Of those that a mesh axis runs over, the one named last changes fastest.
Arguments:
- inputs: bfloat16 [32768, 1536], P(('dp', 'seq')), parts along dimension 0, may hold values from -6 to 6
- lengths: int32 [16], P('dp'), parts along dimension 0, may hold values from 1024 to 2048
- kernel: float32 [31, 1536], replicated, may hold values from -1 to 1
- gain: float32 [1536], replicated, may hold values from 0.5 to 1.5
- q_weight: bfloat16 [1536, 1024], replicated
- k_weight: bfloat16 [1536, 1024], replicated, may hold values from -0.15625 to 0.15625
- v_weight: bfloat16 [1536, 1024], replicated, may hold values from -0.15625 to 0.15625
- grad_attn: bfloat16 [32768, 1024], P(('dp', 'seq')), parts along dimension 0, may hold values from -6 to 6
Outputs:
- attn: bfloat16 [32768, 1024], P(('dp', 'seq')), parts along dimension 0
- grad_input: bfloat16 [32768, 1536], P(('dp', 'seq')), parts along dimension 0
- grad_kernel: float32 [496, 1536], P('dp'), parts along dimension 0
There are 16 independent parts, one for each index of `dp`. A program takes and returns all parts, laid end to end along the dimension named above; an argument that names none is the same for every part. Nothing has to cross between parts.
All inputs are finite; a program needn't handle non-finite values.
Results may differ from a plain program's by a relative error of at most 0.04.
The roundings to bfloat16 on the way count: a program that leaves them out, or rounds other values in their place, can miss the bound.
Values may be sent and summed in bfloat16 or wider, within the bound.
No kernel may reach another device: no remote copies, remote signals or barrier semaphores. Data moves between devices by JAX's collectives and lax.ppermute only.
A program may use at most 128 MiB of HBM per device.

v0:
```python
import jax
import jax.numpy as jnp
from jax import lax
from jax.sharding import PartitionSpec as P

HEADS = 16
HDIM = 64
KSIZE = 31


def with_halo(block, sides, width):
    for axis, dim in sides:
        count = lax.axis_size(axis)
        forward = [(i, i + 1) for i in range(count - 1)]
        backward = [(target, source) for source, target in forward]
        low = lax.ppermute(
            lax.slice_in_dim(block, block.shape[dim] - width, None, axis=dim), axis, forward
        )
        high = lax.ppermute(lax.slice_in_dim(block, 0, width, axis=dim), axis, backward)
        block = jnp.concatenate([low, block, high], axis=dim)
    return block


def head_forward(query, key, value, valid):
    frames = query.shape[0]
    groups = query.shape[1] // HDIM
    block = min(512, frames)
    qblocks = query.reshape(frames // block, block, groups, HDIM)
    keys = key.reshape(frames, groups, HDIM)
    values = value.reshape(frames, groups, HDIM)

    def one_block(qblock):
        scores = jnp.einsum(
            "bgd,lgd->gbl", qblock, keys, preferred_element_type=jnp.float32
        ) * HDIM ** (-0.5)
        scores = jnp.where(valid[None, None, :], scores, -1e30)
        top = jnp.max(scores, axis=-1, keepdims=True)
        expo = jnp.exp(scores - top)
        probs = expo / jnp.sum(expo, axis=-1, keepdims=True)
        weights = probs.astype(jnp.bfloat16)
        return jnp.einsum(
            "gbl,lgd->bgd", weights, values, preferred_element_type=jnp.float32
        ).astype(jnp.bfloat16)

    result = lax.map(one_block, qblocks)
    return result.reshape(frames, groups * HDIM)


def head_backward(query, key, value, dout, valid):
    frames = query.shape[0]
    groups = query.shape[1] // HDIM
    block = min(512, frames)
    qblocks = query.reshape(frames // block, block, groups, HDIM)
    dblocks = dout.reshape(frames // block, block, groups, HDIM)
    keys = key.reshape(frames, groups, HDIM)
    values = value.reshape(frames, groups, HDIM)

    def one_block(carry, pair):
        qblock, dblock = pair
        scores = jnp.einsum(
            "bgd,lgd->gbl", qblock, keys, preferred_element_type=jnp.float32
        ) * HDIM ** (-0.5)
        scores = jnp.where(valid[None, None, :], scores, -1e30)
        top = jnp.max(scores, axis=-1, keepdims=True)
        expo = jnp.exp(scores - top)
        probs = expo / jnp.sum(expo, axis=-1, keepdims=True)
        weights = probs.astype(jnp.bfloat16)
        grad_val = jnp.einsum("gbl,bgd->lgd", weights, dblock, preferred_element_type=jnp.float32)
        dprobs = jnp.einsum("bgd,lgd->gbl", dblock, values, preferred_element_type=jnp.float32)
        delta = jnp.sum(probs * dprobs, axis=-1, keepdims=True)
        dscores = (probs * (dprobs - delta) * HDIM ** (-0.5)).astype(jnp.bfloat16)
        grad_q = jnp.einsum(
            "gbl,lgd->bgd", dscores, keys, preferred_element_type=jnp.float32
        ).astype(jnp.bfloat16)
        grad_k = jnp.einsum("gbl,bgd->lgd", dscores, qblock, preferred_element_type=jnp.float32)
        return ((carry[0] + grad_k, carry[1] + grad_val), grad_q)

    start = (
        jnp.zeros((frames, groups, HDIM), jnp.float32),
        jnp.zeros((frames, groups, HDIM), jnp.float32),
    )
    (grad_k, grad_val), grad_q = lax.scan(one_block, start, (qblocks, dblocks))
    width = groups * HDIM
    return (
        grad_q.reshape(frames, width),
        grad_k.astype(jnp.bfloat16).reshape(frames, width),
        grad_val.astype(jnp.bfloat16).reshape(frames, width),
    )


def local(inputs, lengths, kernel, gain, q_weight, k_weight, v_weight, grad_attn):
    rows = inputs.shape[0]
    half = KSIZE // 2
    devices_seq = lax.axis_size("seq")
    first = lax.axis_index("seq") * rows
    total_frames = rows * devices_seq
    width = HEADS // devices_seq * HDIM
    own_start = lax.axis_index("seq") * width
    positions = first + jnp.arange(rows, dtype=jnp.int32)
    live = (positions < lengths[0]).astype(jnp.bfloat16)[:, None]
    valid = jnp.arange(total_frames, dtype=jnp.int32) < lengths[0]
    masked = inputs * live
    padded = with_halo(masked, (("seq", 0),), half).astype(jnp.float32)
    conv = jnp.zeros((rows, inputs.shape[1]), jnp.float32)
    for tap in range(KSIZE):
        conv = conv + kernel[tap] * padded[tap : tap + rows]
    mixed = inputs.astype(jnp.float32) + conv
    rstd = lax.rsqrt(jnp.mean(mixed * mixed, axis=-1, keepdims=True) + 1e-05)
    normed = (mixed * rstd * gain).astype(jnp.bfloat16)
    all_normed = lax.all_gather(normed, "seq", axis=0, tiled=True)
    q_own = lax.dynamic_slice_in_dim(q_weight, own_start, width, 1)
    k_own = lax.dynamic_slice_in_dim(k_weight, own_start, width, 1)
    v_own = lax.dynamic_slice_in_dim(v_weight, own_start, width, 1)
    q_heads = jnp.dot(all_normed, q_own, preferred_element_type=jnp.float32).astype(jnp.bfloat16)
    k_heads = jnp.dot(all_normed, k_own, preferred_element_type=jnp.float32).astype(jnp.bfloat16)
    v_heads = jnp.dot(all_normed, v_own, preferred_element_type=jnp.float32).astype(jnp.bfloat16)
    out_heads = head_forward(q_heads, k_heads, v_heads, valid)
    heads_out = lax.all_to_all(out_heads, "seq", split_axis=0, concat_axis=1, tiled=True)
    attn = heads_out * live
    dout = grad_attn * live
    dout_heads = lax.all_to_all(dout, "seq", split_axis=1, concat_axis=0, tiled=True)
    grad_qh, grad_kh, grad_vh = head_backward(q_heads, k_heads, v_heads, dout_heads, valid)
    contract = (((1,), (1,)), ((), ()))
    q_own = lax.dynamic_slice_in_dim(q_weight, own_start, width, 1)
    k_own = lax.dynamic_slice_in_dim(k_weight, own_start, width, 1)
    v_own = lax.dynamic_slice_in_dim(v_weight, own_start, width, 1)
    partial_grad = lax.dot_general(grad_qh, q_own, contract, preferred_element_type=jnp.float32)
    partial_grad = partial_grad + lax.dot_general(
        grad_kh, k_own, contract, preferred_element_type=jnp.float32
    )
    partial_grad = partial_grad + lax.dot_general(
        grad_vh, v_own, contract, preferred_element_type=jnp.float32
    )
    grad_normed = lax.psum_scatter(
        partial_grad.astype(jnp.bfloat16), "seq", scatter_dimension=0, tiled=True
    ).astype(jnp.float32)
    scaled = grad_normed * gain
    grad_mixed = rstd * scaled - mixed * rstd**3 * jnp.mean(scaled * mixed, axis=-1, keepdims=True)
    grad_pad = with_halo(grad_mixed.astype(jnp.bfloat16), (("seq", 0),), half).astype(
        grad_mixed.dtype
    )
    back = jnp.zeros_like(grad_mixed)
    taps = []
    for tap in range(KSIZE):
        back = back + kernel[tap] * grad_pad[2 * half - tap : 2 * half - tap + rows]
        taps.append(jnp.sum(grad_mixed * padded[tap : tap + rows], axis=0))
    grad_kernel = lax.psum(jnp.stack(taps, axis=0).astype(jnp.bfloat16), "seq").astype(jnp.float32)
    grad_input = (grad_mixed + live.astype(jnp.float32) * back).astype(jnp.bfloat16)
    return (attn, grad_input, grad_kernel)


def solution(mesh):
    placed = (P(("dp", "seq"), None), P("dp"), P(), P(), P(), P(), P(), P(("dp", "seq"), None))
    return jax.shard_map(
        local,
        mesh=mesh,
        in_specs=placed,
        out_specs=(P(("dp", "seq"), None), P(("dp", "seq"), None), P("dp", None)),
        check_vma=False,
    )
```

profile of v0, /device:TPU:71, one launch (start us, length us, event | category | flops | bytes accessed | tf_op | source)
XLA Modules:
  0.0 638.2 jit_solution(13328002091234281790)
XLA Ops:
  9.7 7.6 %collective-permute-start = (bf16[15,1536]{1,0:T(8,128)(2,1)S(1)}, bf16[15,1536]{1,0:T(8,128)(2,1)S(1)}, u32[]{:S(2)}, u32[]{:S(2)}) collective-permute-start(bf16[15,1536]{1,0:T(8,128)(2,1)S(1)} %get-tuple-element.293), channel_id=1, source_target_pairs={{0,16},{16,32},{32,48},{48,64},{64,80},{80,96},{96,112},{112,128},... | collective-permute-start | bytes 138248 | tf_op jit(solution)/shard_map/ppermute | solution.py:16
  17.2 1.9 collective-permute-start.1
  22.8 3.7 collective-permute-done.1
  26.7 4.5 multiply_reduce_fusion.33
  33.6 89.6 %all-gather.2.cloned.1.call-done = bf16[2048,1536]{1,0:T(8,128)(2,1)} async-done(((bf16[128,1536]{1,0:T(8,128)(2,1)}), bf16[2048,1536]{1,0:T(8,128)(2,1)}) %all-gather.2.cloned.1.call-update) | async-done | bytes 6291472 | tf_op jit(solution)/shard_map/all_gather | solution.py:110
  123.3 4.9 convolution_convert_fusion.3
  130.9 5.8 fusion.45
  136.7 3.1 fusion.44
  140.5 20.7 %while.26 = (s32[]{:T(128)}, bf16[4,512,1,64]{1,3,2,0:T(8,128)(2,1)}, bf16[4,512,1,64]{1,3,2,0:T(8,128)(2,1)}, bf16[2048,1,64]{0,2,1:T(8,128)(2,1)S(1)}, bf16[2048,1,64]{0,2,1:T(8,128)(2,1)}, /*index=5*/s32[]{:T(128)}, s32[]{:T(128)}) while((s32[]{:T(128)}, bf16[4,512,1,64]{1,3,2,0:T(8,128)(2,1)}, ...), condition=%wide.region_4.5_spmd.clone, body=%wide.region_1.4_spmd.clone.sunk | while | flops 281052160 | bytes 14305405 | solution.py:45
  166.5 5.3 all-to-all-start
  173.6 12.2 %all-to-all-done = bf16[16,128,64]{1,2,0:T(8,128)(2,1)} async-done(((bf16[16,128,64]{1,2,0:T(8,128)(2,1)}), bf16[16,128,64]{1,2,0:T(8,128)(2,1)}, u32[]{:S(2)}, u32[]{:S(2)}) %all-to-all-start) | async-done | bytes 262176 | tf_op jit(solution)/shard_map/all_to_all | solution.py:118
  187.6 4.9 all-to-all-start.1
  192.8 12.8 %all-to-all-done.1 = bf16[128,16,64]{0,2,1:T(8,128)(2,1)} async-done(((bf16[128,16,64]{0,2,1:T(8,128)(2,1)}), bf16[128,16,64]{0,2,1:T(8,128)(2,1)}, u32[]{:S(2)}, u32[]{:S(2)}) %all-to-all-start.1) | async-done | bytes 262176 | tf_op jit(solution)/shard_map/all_to_all | solution.py:121
  211.6 46.0 %while.27 = (s32[]{:T(128)}, f32[2048,1,64]{0,2,1:T(8,128)}, f32[2048,1,64]{0,2,1:T(8,128)}, bf16[4,512,1,64]{1,3,2,0:T(8,128)(2,1)}, bf16[4,512,1,64]{1,3,2,0:T...) while((s32[]{:T(128)}, f32[2048,1,64]{0,2,1:T(8,128)}, ...), condition=%wide.region_9.10_spmd.clone, body=%wide.region_5.9_spmd.clone.sunk | while | flops 698909184 | bytes 49383740 | solution.py:82
  258.9 6.5 %fusion.84 = f32[2048,1536]{1,0:T(8,128)} fusion(bf16[2048,64]{0,1:T(8,128)(2,1)S(1)} %bitcast.140, bf16[1536,1024]{1,0:T(8,128)(2,1)S(1)} %copy-done, s32[]{:T(128)S(6)} %select_n.17), kind=kOutput, calls=%fused_computation.167 | convolution fusion | flops 402653184 | bytes 13238276 | tf_op jit(solution)/shard_map/dot_general | solution.py:127
  265.4 7.4 %fusion.81 = f32[2048,1536]{1,0:T(8,128)} fusion(bf16[1536,1024]{1,0:T(8,128)(2,1)} %param.17, s32[]{:T(128)S(6)} %select_n.17, f32[2048,1,64]{0,2,1:T(8,128)S(1)} %copy-done.5), kind=kOutput, calls=%fused_computation.164 | convolution fusion | flops 402784256 | bytes 13500420 | tf_op jit(solution)/shard_map/dot_general | solution.py:128
  272.8 12.3 %add_convert_fusion = bf16[2048,1536]{1,0:T(8,128)(2,1)} fusion(f32[2048,1536]{1,0:T(8,128)} %fusion.84, f32[2048,1536]{1,0:T(8,128)} %fusion.81, bf16[1536,1024]{1,0:T(8,128)(2,1)} %param.18, s32[]{:T(128)S(6)} %select_n.17, f32[2048,1,64]{0,2,1:T(8,128)S(1)} %copy-done.10), kind=kOutput, calls=%fused_computation.53 | convolution fusion | flops 412221440 | bytes 32374788 | tf_op jit(solution)/shard_map/dot_general | solution.py:131
  285.4 113.1 %reduce-scatter.2.cloned.1.call-done = bf16[128,1536]{1,0:T(8,128)(2,1)} async-done(((bf16[2048,1536]{1,0:T(8,128)(2,1)}), bf16[128,1536]{1,0:T(8,128)(2,1)}) %reduce-scatter.2.cloned.1.call-update) | async-done | bytes 393232 | tf_op jit(solution)/shard_map/reduce_scatter | solution.py:134
  400.0 4.1 multiply_reduce_fusion.1
  406.6 5.4 collective-permute-start.2
  412.1 1.9 collective-permute-start.3
  455.2 5.9 stack.159
  462.2 4.9 fusion.49
  467.1 163.0 %all-reduce.2.cloned.1.call-done = bf16[31,1536]{1,0:T(8,128)(2,1)} async-done(((bf16[31,1536]{1,0:T(8,128)(2,1)}), bf16[31,1536]{1,0:T(8,128)(2,1)}) %all-reduce.2.cloned.1.call-update) | async-done | bytes 95248 | tf_op jit(solution)/shard_map/psum | solution.py:147
  (270 shorter events, 141.6 us)
Async XLA Ops:
  7.2 116.1 %copy-start = (bf16[1536,1024]{1,0:T(8,128)(2,1)S(1)}, bf16[1536,1024]{1,0:T(8,128)(2,1)}, u32[]{:S(2)}) copy-start(bf16[1536,1024]{1,0:T(8,128)(2,1)} %param.16) | copy-start | bytes 9437188
  7.2 116.1 %all-gather.2.cloned.1.call-start = ((), (), s32[]{:S(2)}) async-start(), calls=%async_computation.3 | async-start | bytes 6684672 | tf_op jit(solution)/shard_map/all_gather | solution.py:110
  9.7 13.2 %collective-permute-start = (bf16[15,1536]{1,0:T(8,128)(2,1)S(1)}, bf16[15,1536]{1,0:T(8,128)(2,1)S(1)}, u32[]{:S(2)}, u32[]{:S(2)}) collective-permute-start(bf16[15,1536]{1,0:T(8,128)(2,1)S(1)} %get-tuple-element.293), channel_id=1, source_target_pairs={{0,16},{16,32},{32,48},{48,64},{64,80},{80,96},{96,112},{112,128},... | collective-permute-start | bytes 138248 | tf_op jit(solution)/shard_map/ppermute | solution.py:16
  17.2 9.3 %collective-permute-start.1 = (bf16[15,1536]{1,0:T(8,128)(2,1)S(1)}, bf16[15,1536]{1,0:T(8,128)(2,1)S(1)}, u32[]{:S(2)}, u32[]{:S(2)}) collective-permute-start(bf16[15,1536]{1,0:T(8,128)(2,1)S(1)} %get-tuple-element.294), channel_id=1, source_target_pairs={{16,0},{32,16},{48,32},{64,48},{80,64},{96,80},{112,96},{128,112},... | collective-permute-start | bytes 138248 | tf_op jit(solution)/shard_map/ppermute | solution.py:19
  21.0 10.2 %copy-start.16 = (f32[1536]{0:T(1024)}, f32[1536]{0:T(1024)S(1)}, u32[]{:S(2)}) copy-start(f32[1536]{0:T(1024)S(1)} %get-tuple-element.218) | copy-start | bytes 18436
  21.0 10.2 %copy-start.18 = (f32[1536]{0:T(1024)}, f32[1536]{0:T(1024)S(1)}, u32[]{:S(2)}) copy-start(f32[1536]{0:T(1024)S(1)} %get-tuple-element.219) | copy-start | bytes 18436
  21.0 10.2 %copy-start.20 = (f32[1536]{0:T(1024)}, f32[1536]{0:T(1024)S(1)}, u32[]{:S(2)}) copy-start(f32[1536]{0:T(1024)S(1)} %get-tuple-element.220) | copy-start | bytes 18436
  21.0 10.2 %copy-start.21 = (f32[1536]{0:T(1024)}, f32[1536]{0:T(1024)S(1)}, u32[]{:S(2)}) copy-start(f32[1536]{0:T(1024)S(1)} %get-tuple-element.221) | copy-start | bytes 18436
  21.0 10.2 %copy-start.22 = (f32[1536]{0:T(1024)}, f32[1536]{0:T(1024)S(1)}, u32[]{:S(2)}) copy-start(f32[1536]{0:T(1024)S(1)} %get-tuple-element.222) | copy-start | bytes 18436
  21.0 10.2 %copy-start.23 = (f32[1536]{0:T(1024)}, f32[1536]{0:T(1024)S(1)}, u32[]{:S(2)}) copy-start(f32[1536]{0:T(1024)S(1)} %get-tuple-element.223) | copy-start | bytes 18436
  21.1 10.2 %copy-start.24 = (f32[1536]{0:T(1024)}, f32[1536]{0:T(1024)S(1)}, u32[]{:S(2)}) copy-start(f32[1536]{0:T(1024)S(1)} %get-tuple-element.224) | copy-start | bytes 18436
  21.1 10.2 %copy-start.25 = (f32[1536]{0:T(1024)}, f32[1536]{0:T(1024)S(1)}, u32[]{:S(2)}) copy-start(f32[1536]{0:T(1024)S(1)} %get-tuple-element.225) | copy-start | bytes 18436
  21.1 10.2 %copy-start.26 = (f32[1536]{0:T(1024)}, f32[1536]{0:T(1024)S(1)}, u32[]{:S(2)}) copy-start(f32[1536]{0:T(1024)S(1)} %get-tuple-element.226) | copy-start | bytes 18436
  166.5 19.3 %all-to-all-start = ((bf16[16,128,64]{1,2,0:T(8,128)(2,1)}), bf16[16,128,64]{1,2,0:T(8,128)(2,1)}, u32[]{:S(2)}, u32[]{:S(2)}) async-start(bf16[16,128,64]{1,2,0:T(8,128)(2,1)} %copy.29), calls=%async_computation | async-start | bytes 524288 | tf_op jit(solution)/shard_map/all_to_all | solution.py:118
  187.6 17.9 %all-to-all-start.1 = ((bf16[128,16,64]{0,2,1:T(8,128)(2,1)}), bf16[128,16,64]{0,2,1:T(8,128)(2,1)}, u32[]{:S(2)}, u32[]{:S(2)}) async-start(bf16[128,16,64]{0,2,1:T(8,128)(2,1)} %bitcast.142), calls=%async_computation.1 | async-start | bytes 524288 | tf_op jit(solution)/shard_map/all_to_all | solution.py:121
  192.5 205.9 %reduce-scatter.2.cloned.1.call-start = ((), (), s32[]{:S(2)}) async-start(), calls=%async_computation.4 | async-start | bytes 6684672 | tf_op jit(solution)/shard_map/reduce_scatter | solution.py:134
  285.1 113.4 %copy-start.15 = (f32[1536]{0:T(1024)S(1)}, f32[1536]{0:T(1024)}, u32[]{:S(2)}) copy-start(f32[1536]{0:T(1024)} %param.15) | copy-start | bytes 18436
  285.1 114.9 %copy-start.50 = (f32[128]{0:T(128)S(1)}, f32[128]{0:T(128)}, u32[]{:S(2)}) copy-start(f32[128]{0:T(128)} %copy-done.49) | copy-start | bytes 1540
  285.1 114.9 %copy-start.51 = (f32[128]{0:T(128)S(1)}, f32[128]{0:T(128)}, u32[]{:S(2)}) copy-start(f32[128]{0:T(128)} %get-tuple-element.295) | copy-start | bytes 1540
  285.1 345.0 %all-reduce.2.cloned.1.call-start = ((), (), s32[]{:S(2)}) async-start(), calls=%async_computation.5 | async-start | bytes 196608 | tf_op jit(solution)/shard_map/psum | solution.py:147
  404.1 58.0 %copy-start.17 = (f32[1536]{0:T(1024)S(1)}, f32[1536]{0:T(1024)}, u32[]{:S(2)}) copy-start(f32[1536]{0:T(1024)} %copy-done.16) | copy-start | bytes 18436
  404.1 58.0 %copy-start.19 = (f32[1536]{0:T(1024)S(1)}, f32[1536]{0:T(1024)}, u32[]{:S(2)}) copy-start(f32[1536]{0:T(1024)} %copy-done.18) | copy-start | bytes 18436
  406.6 54.6 %collective-permute-start.2 = (bf16[15,1536]{1,0:T(8,128)(2,1)}, bf16[15,1536]{1,0:T(8,128)(2,1)}, u32[]{:S(2)}, u32[]{:S(2)}) collective-permute-start(bf16[15,1536]{1,0:T(8,128)(2,1)} %get-tuple-element.291), channel_id=1, source_target_pairs={{0,16},{16,32},{32,48},{48,64},{64,80},{80,96},{96,112},{112,128},... | collective-permute-start | bytes 138248 | tf_op jit(solution)/shard_map/ppermute | solution.py:16
  412.1 49.1 %collective-permute-start.3 = (bf16[15,1536]{1,0:T(8,128)(2,1)}, bf16[15,1536]{1,0:T(8,128)(2,1)}, u32[]{:S(2)}, u32[]{:S(2)}) collective-permute-start(bf16[15,1536]{1,0:T(8,128)(2,1)} %get-tuple-element.292), channel_id=1, source_target_pairs={{16,0},{32,16},{48,32},{64,48},{80,64},{96,80},{112,96},{128,112},... | collective-permute-start | bytes 138248 | tf_op jit(solution)/shard_map/ppermute | solution.py:19
  (60 other events, 308.6 us)
Sparse Core Ops, SparseCore 0:
  33.8 89.4 all-gather.1
  285.3 113.1 reduce-scatter.1
  461.3 168.7 all-reduce.1
where the time goes:
time: 645 us; the launch traced here: 638 us
  waiting for transfers between devices  395 us (61%)
  matrix products  83.3 us (13%)
  local copies, waits for them, and re-layouts  73.2 us (11%)
  other arithmetic  43.9 us (7%)
  starting transfers between devices  27.6 us (4%)
  between operations  15.3 us (2%)
    psum x1, waiting for transfers between devices, local(): lax.psum(jnp.stack(taps, axis=0).astype(jnp.bfloat16), 'seq')  163 us
    reduce_scatter x1, waiting for transfers between devices, local(): lax.psum_scatter(partial_grad.astype(jnp.bfloat16), 'seq', scatter_dimens...  113 us
    all_gather x1, waiting for transfers between devices, local(): all_normed = lax.all_gather(normed, 'seq', axis=0, tiled=True)  89.6 us
    another operation x32, local copies, waits for them, and re-layouts, local(): jnp.stack(taps, axis=0).astype(jnp.bfloat16)  45.4 us
    dot_general x8, matrix products, one_block(): jnp.einsum('bgd,lgd->gbl', qblock, keys, preferred_element_type=jnp.float32)  13.9 us
    ppermute x2, starting transfers between devices, with_halo(): lax.ppermute(lax.slice_in_dim(block, block.shape[dim] - width, None, axis...  13 us
  transfers between devices with their start and end apart: 9, of which 6 were waited for; matrix products, arithmetic and copies ran while one was open for 9% of the time, Pallas kernels for 0%

commit v1 on v0

v1 whole, which is shorter than its diff:
```python
import functools
import math

import jax
import jax.numpy as jnp
from jax import lax
from jax.experimental import pallas as pl
from jax.experimental.pallas import tpu as pltpu
from jax.sharding import PartitionSpec as P

HEADS = 16
HDIM = 64
KSIZE = 31
PAD = 16
LANES = 128
BF = jnp.bfloat16
F32 = jnp.float32
VMEM = pl.BlockSpec(memory_space=pltpu.VMEM)
SMEM = pl.BlockSpec(memory_space=pltpu.SMEM)
ANY = pl.BlockSpec(memory_space=pl.ANY)


def live_rows(first, rows, length):
    pos = first + lax.broadcasted_iota(jnp.int32, (rows, LANES), 0)
    return (pos < length).astype(F32)


def padded_chunk(lo_ref, x_ref, hi_ref, lanes, mask):
    whole = jnp.concatenate(
        [lo_ref[:, lanes], x_ref[:, lanes], hi_ref[:, lanes]], axis=0
    ).astype(F32)
    return whole * mask if mask is not None else whole


def conv_chunk(padded, taps_ref, lanes, rows, reverse):
    total = None
    for r in range(8):
        acc = None
        for a in range(4):
            o = 8 * a + r
            if o == 0:
                continue
            j = KSIZE - o if reverse else o - 1
            term = taps_ref[j : j + 1, lanes] * padded[8 * a : 8 * a + rows + 8]
            acc = term if acc is None else acc + term
        part = acc[r : r + rows]
        total = part if total is None else total + part
    return total


def chunk(c):
    return pl.ds(pl.multiple_of(c * LANES, LANES), LANES)


def pre_kernel(
    len_ref, first_ref, x_ref, lo_ref, hi_ref, taps_ref, gain_ref, g_ref, wq_ref, wk_ref, wv_ref,
    send_ref, mixed_ref, rstd_ref, w_scr, n_scr, sems,
):
    rows, width = x_ref.shape
    copies = [
        pltpu.make_async_copy(w, w_scr.at[i], sems.at[i])
        for i, w in enumerate((wq_ref, wk_ref, wv_ref))
    ]
    for cp in copies:
        cp.start()
    length = len_ref[0]
    first = first_ref[0]
    mask = live_rows(first - PAD, rows + 2 * PAD, length)

    def conv_step(c, sq):
        lanes = chunk(c)
        padded = padded_chunk(lo_ref, x_ref, hi_ref, lanes, mask)
        conv = conv_chunk(padded, taps_ref, lanes, rows, False)
        mixed = x_ref[:, lanes].astype(F32) + conv
        mixed_ref[:, lanes] = mixed
        return sq + mixed * mixed

    sq = lax.fori_loop(0, width // LANES, conv_step, jnp.zeros((rows, LANES), F32))
    rstd = lax.rsqrt(jnp.sum(sq, axis=-1, keepdims=True) / width + 1e-05)
    rstd_ref[...] = jnp.broadcast_to(rstd, (rows, LANES))
    n_scr[...] = (mixed_ref[...] * rstd * gain_ref[...]).astype(BF)
    live = live_rows(first, rows, length)[:, :HDIM]
    for h in range(HEADS):
        dout = g_ref[:, h * HDIM : (h + 1) * HDIM].astype(F32) * live
        send_ref[h, :, HDIM : 2 * HDIM] = dout.astype(BF)
    for i, at in enumerate((0, 2 * HDIM, 3 * HDIM)):
        copies[i].wait()
        heads = jnp.dot(n_scr[...], w_scr[i], preferred_element_type=F32).astype(BF)
        for h in range(HEADS):
            send_ref[h, :, at : at + HDIM] = heads[:, h * HDIM : (h + 1) * HDIM]


def attn_kernel(len_ref, in_ref, out_ref, kvt_scr, s_scr, e_scr, d_scr, acc_scr, *, block, step):
    frames = in_ref.shape[0]
    length = len_ref[0]
    scale = HDIM ** (-0.5)
    factor = scale * math.log2(math.e)
    half = frames // 2
    kv = in_ref.at[:, 2 * HDIM : 4 * HDIM]
    kvt_scr[...] = kv[...].T
    acc_scr[...] = jnp.zeros_like(acc_scr)
    lane = lax.broadcasted_iota(jnp.int32, (block, LANES), 1)
    nt = (((1,), (1,)), ((), ()))
    steps = frames // step

    def one_block(b, _):
        rows = pl.ds(pl.multiple_of(b * block, block), block)
        qd = in_ref[rows, 0 : 2 * HDIM]
        zero = jnp.zeros_like(qd)
        q0 = jnp.where(lane < HDIM, qd, zero)
        d0 = jnp.where(lane < HDIM, zero, qd)
        top = None
        for i in range(steps):
            keys = slice(i * step, (i + 1) * step)
            s = lax.dot_general(kv[keys, :], q0, nt, preferred_element_type=F32)
            if (i + 1) * step > half:
                pos = i * step + lax.broadcasted_iota(jnp.int32, (step, block), 0)
                s = jnp.where(pos < length, s, -1e30)
            s_scr[keys, :] = s
            part = jnp.max(s.reshape(step // 8, 8, block), axis=0)
            top = part if top is None else jnp.maximum(top, part)
        top = jnp.max(top, axis=0, keepdims=True)
        total = jnp.zeros((8, block), F32)
        out = jnp.zeros((HDIM, block), F32)
        for i in range(steps):
            keys = slice(i * step, (i + 1) * step)
            e = jnp.exp2((s_scr[keys, :] - top) * factor)
            s_scr[keys, :] = e
            eb = e.astype(BF)
            e_scr[keys, :] = eb
            total = total + jnp.sum(e.reshape(step // 8, 8, block), axis=0)
            out = out + jnp.dot(kvt_scr[HDIM:, keys], eb, preferred_element_type=F32)
        inv = 1.0 / jnp.sum(total, axis=0, keepdims=True)
        out = out * inv
        dt = d0.astype(F32).T[HDIM:, :] * inv
        delta = jnp.sum(dt * out, axis=0, keepdims=True)
        dsc = jnp.concatenate([jnp.zeros((HDIM, block), F32), dt], axis=0)
        d0s = dsc.T.astype(BF)
        gq = jnp.zeros((HDIM, block), F32)
        for i in range(steps):
            keys = slice(i * step, (i + 1) * step)
            dp = lax.dot_general(kv[keys, :], d0s, nt, preferred_element_type=F32)
            ds = (s_scr[keys, :] * (dp - delta)).astype(BF)
            gq = gq + jnp.dot(kvt_scr[:HDIM, keys], ds, preferred_element_type=F32)
            acc_scr[keys, :] += jnp.dot(ds, q0, preferred_element_type=F32) + jnp.dot(
                e_scr[keys, :], d0s, preferred_element_type=F32
            )
        both = jnp.concatenate([out, gq * scale], axis=0)
        out_ref[rows, 2 * HDIM : 4 * HDIM] = both.T.astype(BF)
        return 0

    lax.fori_loop(0, frames // block, one_block, 0)
    lane = lax.broadcasted_iota(jnp.int32, (1, LANES), 1)
    fix = jnp.where(lane < HDIM, scale, 1.0)
    out_ref[:, 0 : 2 * HDIM] = (acc_scr[...] * fix).astype(BF)


def back_kernel(
    in_ref, wq_ref, wk_ref, wv_ref, mixed_ref, rstd_ref, gain_ref, gm_ref, first_ref, last_ref
):
    rows, width = mixed_ref.shape
    nt = (((1,), (1,)), ((), ()))
    grad = None
    for w_ref, at in ((wq_ref, 3 * HDIM), (wk_ref, 0), (wv_ref, HDIM)):
        feats = jnp.concatenate([in_ref[h, :, at : at + HDIM] for h in range(HEADS)], axis=1)
        part = lax.dot_general(feats, w_ref[...], nt, preferred_element_type=F32)
        grad = part if grad is None else grad + part
    scaled = grad * gain_ref[...]
    mixed = mixed_ref[...]
    rstd = rstd_ref[:, 0:1]
    mean = jnp.sum(scaled * mixed, axis=-1, keepdims=True) / width
    gm = rstd * scaled - mixed * (rstd * rstd * rstd * mean)
    gm_ref[...] = gm
    first_ref[...] = gm[:PAD].astype(BF)
    last_ref[...] = gm[rows - PAD :].astype(BF)


def taps_kernel(len_ref, first_ref, x_ref, lo_ref, hi_ref, gm_ref, out_ref):
    rows, width = x_ref.shape
    mask = live_rows(first_ref[0] - PAD, rows + 2 * PAD, len_ref[0])

    def step(c, _):
        lanes = chunk(c)
        padded = padded_chunk(lo_ref, x_ref, hi_ref, lanes, mask)
        gm = gm_ref[:, lanes]
        result = [None] * (KSIZE + 1)
        for r in range(8):
            fill = [jnp.zeros((r, LANES), F32)] if r else []
            ext = jnp.concatenate(fill + [gm, jnp.zeros((8 - r, LANES), F32)], axis=0)
            for a in range(4):
                o = 8 * a + r
                if o == 0:
                    continue
                prod = ext * padded[8 * a : 8 * a + rows + 8]
                result[o - 1] = jnp.sum(prod, axis=0, keepdims=True)
        result[KSIZE] = jnp.zeros((1, LANES), F32)
        out_ref[:, lanes] = jnp.concatenate(result, axis=0).astype(BF)
        return 0

    lax.fori_loop(0, width // LANES, step, 0)


def final_kernel(len_ref, first_ref, in_ref, gm_ref, lo_ref, hi_ref, taps_ref, attn_ref, gi_ref):
    rows, width = gm_ref.shape
    live = live_rows(first_ref[0], rows, len_ref[0])

    def step(c, _):
        lanes = chunk(c)
        gm = gm_ref[:, lanes]
        padded = jnp.concatenate(
            [lo_ref[:, lanes].astype(F32), gm, hi_ref[:, lanes].astype(F32)], axis=0
        )
        back = conv_chunk(padded, taps_ref, lanes, rows, True)
        gi_ref[:, lanes] = (gm + live * back).astype(BF)
        return 0

    lax.fori_loop(0, width // LANES, step, 0)
    for h in range(HEADS):
        out = in_ref[h, :, 2 * HDIM : 3 * HDIM].astype(F32) * live[:, :HDIM]
        attn_ref[:, h * HDIM : (h + 1) * HDIM] = out.astype(BF)


def params(mib):
    return pltpu.CompilerParams(vmem_limit_bytes=mib << 20)


def halo(low, high):
    count = lax.axis_size("seq")
    forward = [(i, i + 1) for i in range(count - 1)]
    backward = [(i + 1, i) for i in range(count - 1)]
    return lax.ppermute(low, "seq", forward), lax.ppermute(high, "seq", backward)


def local(inputs, lengths, kernel, gain, q_weight, k_weight, v_weight, grad_attn):
    rows, width = inputs.shape
    count = lax.axis_size("seq")
    frames = rows * count
    feats = HEADS * HDIM
    sds = jax.ShapeDtypeStruct
    first = (lax.axis_index("seq") * rows).astype(jnp.int32).reshape(1)
    gain = gain.reshape(1, width)
    lo, hi = halo(inputs[rows - PAD :], inputs[:PAD])

    send, mixed, rstd = pl.pallas_call(
        pre_kernel,
        name="pre",
        out_shape=(
            sds((HEADS, rows, 4 * HDIM), BF),
            sds((rows, width), F32),
            sds((rows, LANES), F32),
        ),
        in_specs=[SMEM, SMEM] + [VMEM] * 6 + [ANY] * 3,
        out_specs=(VMEM,) * 3,
        scratch_shapes=[
            pltpu.VMEM((3, width, feats), BF),
            pltpu.VMEM((rows, width), BF),
            pltpu.SemaphoreType.DMA((3,)),
        ],
        compiler_params=params(24),
    )(lengths, first, inputs, lo, hi, kernel, gain, grad_attn, q_weight, k_weight, v_weight)

    heads_in = lax.all_to_all(send, "seq", split_axis=0, concat_axis=0, tiled=True)
    block, step = 256, 256
    heads_out = pl.pallas_call(
        functools.partial(attn_kernel, block=block, step=step),
        name="attn",
        out_shape=sds((frames, 4 * HDIM), BF),
        in_specs=[SMEM, VMEM],
        out_specs=VMEM,
        scratch_shapes=[
            pltpu.VMEM((2 * HDIM, frames), BF),
            pltpu.VMEM((frames, block), F32),
            pltpu.VMEM((frames, block), BF),
            pltpu.VMEM((frames, block), BF),
            pltpu.VMEM((frames, LANES), F32),
        ],
        compiler_params=params(24),
    )(lengths, heads_in.reshape(frames, 4 * HDIM))
    grads = lax.all_to_all(
        heads_out.reshape(HEADS, rows, 4 * HDIM), "seq", split_axis=0, concat_axis=0, tiled=True
    )

    gm, gm_first, gm_last = pl.pallas_call(
        back_kernel,
        name="back",
        out_shape=(sds((rows, width), F32), sds((PAD, width), BF), sds((PAD, width), BF)),
        in_specs=[VMEM] * 7,
        out_specs=(VMEM,) * 3,
        compiler_params=params(24),
    )(grads, q_weight, k_weight, v_weight, mixed, rstd, gain)
    gm_lo, gm_hi = halo(gm_last, gm_first)
    taps = pl.pallas_call(
        taps_kernel,
        name="taps",
        out_shape=sds((KSIZE + 1, width), BF),
        in_specs=[SMEM, SMEM] + [VMEM] * 4,
        out_specs=VMEM,
        compiler_params=params(24),
    )(lengths, first, inputs, lo, hi, gm)
    total = taps.astype(F32)
    for bit in (1, 4, 8, 2):
        pairs = [(i, i ^ bit) for i in range(count)]
        mine = total.astype(BF)
        total = mine.astype(F32) + lax.ppermute(mine, "seq", pairs).astype(F32)
    attn, grad_input = pl.pallas_call(
        final_kernel,
        name="final",
        out_shape=(sds((rows, feats), BF), sds((rows, width), BF)),
        in_specs=[SMEM, SMEM] + [VMEM] * 5,
        out_specs=(VMEM,) * 2,
        compiler_params=params(24),
    )(lengths, first, grads, gm, gm_lo, gm_hi, kernel)
    return (attn, grad_input, total[:KSIZE])


def solution(mesh):
    placed = (P(("dp", "seq"), None), P("dp"), P(), P(), P(), P(), P(), P(("dp", "seq"), None))
    return jax.shard_map(
        local,
        mesh=mesh,
        in_specs=placed,
        out_specs=(P(("dp", "seq"), None), P(("dp", "seq"), None), P("dp", None)),
        check_vma=False,
    )
```

time: 645 us -> 167 us (0.26)
  waiting for transfers between devices: 395 us -> 16.7 us
  matrix products: 83.3 us -> 0 us
  blocking collectives: 0 us -> 74.7 us
  local copies, waits for them, and re-layouts: 73.2 us -> 10.1 us
  other arithmetic: 43.9 us -> 0.78 us
  Pallas kernels: 0 us -> 39.6 us
  between operations: 15.3 us -> 1.44 us
    psum x1 -> x0, waiting for transfers between devices: 163 us -> none  [local(): lax.psum(jnp.stack(taps, axis=0).astype(jnp.bfloat16), 'seq')]
    reduce_scatter x1 -> x0, waiting for transfers between devices: 113 us -> none  [local(): lax.psum_scatter(partial_grad.astype(jnp.bfloat16), 'seq', scatter_dimens...]
    all_gather x1 -> x0, waiting for transfers between devices: 89.6 us -> none  [local(): all_normed = lax.all_gather(normed, 'seq', axis=0, tiled=True)]
    dot_general x34 -> x0, matrix products: 83.3 us -> none  [the longest x8 13.9 us: one_block(): jnp.einsum('bgd,lgd->gbl', qblock, keys, preferred_element_type=jnp.float32)]
    all_to_all x0 -> x2, blocking collectives: none -> 74.7 us  [the longest x1 41.8 us: local(): lax.all_to_all(send, 'seq', split_axis=0, concat_axis=0, tiled=True)]
    another operation x34 -> x0, local copies, waits for them, and re-layouts: 46.8 us -> none  [the longest x32 45.4 us: local(): jnp.stack(taps, axis=0).astype(jnp.bfloat16)]
    pallas_call x0 -> x5, Pallas kernels: none -> 39.6 us  [the longest x1 24.8 us: local(): pl.pallas_call(functools.partial(attn_kernel, block=block, step=step), na...]
    all_to_all x2 -> x0, waiting for transfers between devices: 25 us -> none  [the longest x1 12.8 us: local(): lax.all_to_all(dout, 'seq', split_axis=1, concat_axis=0, tiled=True)]
  transfers between devices with their start and end apart: 9 -> 8, of which waited for: 6 -> 4; matrix products, arithmetic and copies ran while one was open for 9% -> 0% of each run, Pallas kernels for 0% -> 2%
where the time goes in v1:
time: 167 us; the launch traced here: 166 us
  blocking collectives  74.7 us (45%)
  Pallas kernels  39.6 us (24%)
  starting transfers between devices  22.6 us (14%)
  waiting for transfers between devices  16.7 us (10%)
  local copies, waits for them, and re-layouts  10.1 us (6%)
    all_to_all x1, blocking collectives, local(): lax.all_to_all(send, 'seq', split_axis=0, concat_axis=0, tiled=True)  41.8 us
    all_to_all x1, blocking collectives, local(): lax.all_to_all(heads_out.reshape(HEADS, rows, 4 * HDIM), 'seq', split_axi...  32.9 us
    pallas_call x1, Pallas kernels, local(): pl.pallas_call(functools.partial(attn_kernel, block=block, step=step), na...  24.8 us
    ppermute x2, starting transfers between devices, halo(): lax.ppermute(low, 'seq', forward)  16.7 us
    ppermute x4, waiting for transfers between devices, local(): total = mine.astype(F32) + lax.ppermute(mine, 'seq', pairs).astype(F32)  9.35 us
    unnamed x22, local copies, waits for them, and re-layouts  8.56 us
    ppermute x2, waiting for transfers between devices, halo(): lax.ppermute(high, 'seq', backward)  7.38 us
    pallas_call x1, Pallas kernels, local(): pl.pallas_call(pre_kernel, name='pre', out_shape=(sds((HEADS, rows, 4 * H...  5.47 us
  transfers between devices with their start and end apart: 8, of which 4 were waited for; matrix products, arithmetic and copies ran while one was open for 0% of the time, Pallas kernels for 2%

profile of v1, /device:TPU:71, one launch (start us, length us, event | category | flops | bytes accessed | tf_op | source)
XLA Modules:
  0.0 165.9 jit_solution(8291231403609797383)
XLA Ops:
  0.6 0.8 fusion
  1.5 2.6 %collective-permute-start.1 = (bf16[16,1536]{1,0:T(8,128)(2,1)S(1)}, bf16[16,1536]{1,0:T(8,128)(2,1)S(1)}, u32[]{:S(2)}, u32[]{:S(2)}) collective-permute-start(bf16[16,1536]{1,0:T(8,128)(2,1)S(1)} %get-tuple-element.19), channel_id=1, source_target_pairs={{16,0},{32,16},{48,32},{64,48},{80,64},{96,80},{112,96},{128,112},... | collective-permute-start | bytes 147464 | tf_op jit(solution)/shard_map/ppermute | solution.py:231
  4.0 6.9 %collective-permute-start = (bf16[16,1536]{1,0:T(8,128)(2,1)S(1)}, bf16[16,1536]{1,0:T(8,128)(2,1)S(1)}, u32[]{:S(2)}, u32[]{:S(2)}) collective-permute-start(bf16[16,1536]{1,0:T(8,128)(2,1)S(1)} %get-tuple-element.20), channel_id=1, source_target_pairs={{0,16},{16,32},{32,48},{48,64},{64,80},{80,96},{96,112},{112,128},... | collective-permute-start | bytes 147464 | tf_op jit(solution)/shard_map/ppermute | solution.py:231
  11.6 0.7 reshape.19.gain_ref
  12.3 1.9 %copy-done = bf16[1536,1024]{1,0:T(8,128)(2,1)S(1)} copy-done((bf16[1536,1024]{1,0:T(8,128)(2,1)S(1)}, bf16[1536,1024]{1,0:T(8,128)(2,1)}, u32[]{:S(2)}) %copy-start) | copy-done | bytes 3145752
  14.2 1.9 %copy-done.2 = bf16[1536,1024]{1,0:T(8,128)(2,1)S(1)} copy-done((bf16[1536,1024]{1,0:T(8,128)(2,1)S(1)}, bf16[1536,1024]{1,0:T(8,128)(2,1)}, u32[]{:S(2)}) %copy-start.2) | copy-done | bytes 3145752
  16.1 1.9 %copy-done.4 = bf16[1536,1024]{1,0:T(8,128)(2,1)S(1)} copy-done((bf16[1536,1024]{1,0:T(8,128)(2,1)S(1)}, bf16[1536,1024]{1,0:T(8,128)(2,1)}, u32[]{:S(2)}) %copy-start.4) | copy-done | bytes 3145752
  18.0 1.0 copy-done.6
  19.0 0.9 copy-done.8
  19.9 0.9 copy-done.10
  20.9 5.5 %pre.1 = (bf16[16,128,256]{2,1,0:T(8,128)(2,1)S(1)}, f32[128,1536]{1,0:T(8,128)S(1)}, f32[128,128]{1,0:T(8,128)S(1)}) custom-call(s32[1]{0:T(128)S(6)} %copy.11.len_ref, s32[1]{0:T(128)} %bitcast.first_ref, bf16[128,1536]{1,0:T(8,128)(2,1)S(1)} %copy-done.6, bf16[16,1536]{1,0:T(8,128)(2,1)S(1)} %collective-permute-done.lo_ref, ...), custom_call_target="tpu_custom_call" | custom-call | tf_op jit(solution)/shard_map/pre/pallas_call | solution.py:244
  26.4 41.8 %all_to_all.10 = bf16[16,128,256]{2,1,0:T(8,128)(2,1)S(1)} all-to-all(bf16[16,128,256]{2,1,0:T(8,128)(2,1)S(1)} %get-tuple-element.11), channel_id=1, replica_groups=mesh['seq'=16,'dp'=16] {'seq'}, dimensions={0} | all-to-all | bytes 2097152 | tf_op jit(solution)/shard_map/all_to_all | solution.py:262
  68.2 24.8 %attn.1 = bf16[2048,256]{1,0:T(8,128)(2,1)S(1)} custom-call(s32[1]{0:T(128)S(6)} %copy.11.len_ref, bf16[2048,256]{1,0:T(8,128)(2,1)S(1)} %bitcast.3), custom_call_target="tpu_custom_call" | custom-call | tf_op jit(solution)/shard_map/attn/pallas_call | solution.py:264
  93.0 32.9 %all_to_all.11.in_ref = bf16[16,128,256]{2,1,0:T(8,128)(2,1)S(1)} all-to-all(bf16[16,128,256]{2,1,0:T(8,128)(2,1)S(1)} %bitcast.4), channel_id=1, replica_groups=mesh['seq'=16,'dp'=16] {'seq'}, dimensions={0} | all-to-all | bytes 2097152 | tf_op jit(solution)/shard_map/all_to_all | solution.py:279
  125.9 3.4 %back.1 = (f32[128,1536]{1,0:T(8,128)S(1)}, bf16[16,1536]{1,0:T(8,128)(2,1)S(1)}, bf16[16,1536]{1,0:T(8,128)(2,1)S(1)}) custom-call(bf16[16,128,256]{2,1,0:T(8,128)(2,1)S(1)} %all_to_all.11.in_ref, bf16[1536,1024]{1,0:T(8,128)(2,1)S(1)} %copy-done.1, bf16[1536,1024]{1,0:T(8,128)(2,1)S(1)} %copy-done.3, bf16[1536,1024]{1,0:T(8,128)(2,1)S(1)} %copy-done.5, ...), custom_call_target="tpu_custom_call" | custom-call | tf_op jit(solution)/shard_map/back/pallas_call | solution.py:283
  129.3 2.7 %taps.1 = bf16[32,1536]{1,0:T(8,128)(2,1)S(1)} custom-call(s32[1]{0:T(128)S(6)} %copy.11.len_ref, s32[1]{0:T(128)} %bitcast.first_ref, bf16[128,1536]{1,0:T(8,128)(2,1)S(1)} %copy-done.7, bf16[16,1536]{1,0:T(8,128)(2,1)S(1)} %collective-permute-done.lo_ref, bf16[16,1536]{1,0:T(8,128)(2,1)S(1)} %collective-permute-done.1.hi_ref, ...), custom_call_target="tpu_custom_call" | custom-call | tf_op jit(solution)/shard_map/taps/pallas_call | solution.py:292
  132.6 0.9 collective-permute-done.4
  133.6 4.0 %collective-permute-done.5 = bf16[32,1536]{1,0:T(8,128)(2,1)S(1)} collective-permute-done((bf16[32,1536]{1,0:T(8,128)(2,1)S(1)}, bf16[32,1536]{1,0:T(8,128)(2,1)S(1)}, u32[]{:S(2)}, u32[]{:S(2)}) %collective-permute-start.5) | collective-permute-done | bytes 98336 | tf_op jit(solution)/shard_map/ppermute | solution.py:304
  138.3 4.4 %collective-permute-done.6 = bf16[32,1536]{1,0:T(8,128)(2,1)S(1)} collective-permute-done((bf16[32,1536]{1,0:T(8,128)(2,1)S(1)}, bf16[32,1536]{1,0:T(8,128)(2,1)S(1)}, u32[]{:S(2)}, u32[]{:S(2)}) %collective-permute-start.6) | collective-permute-done | bytes 98336 | tf_op jit(solution)/shard_map/ppermute | solution.py:304
  142.9 9.8 %collective-permute-start.2 = (bf16[16,1536]{1,0:T(8,128)(2,1)S(1)}, bf16[16,1536]{1,0:T(8,128)(2,1)S(1)}, u32[]{:S(2)}, u32[]{:S(2)}) collective-permute-start(bf16[16,1536]{1,0:T(8,128)(2,1)S(1)} %get-tuple-element.15), channel_id=1, source_target_pairs={{0,16},{16,32},{32,48},{48,64},{64,80},{80,96},{96,112},{112,128},... | collective-permute-start | bytes 147464 | tf_op jit(solution)/shard_map/ppermute | solution.py:231
  152.6 1.9 %collective-permute-start.3 = (bf16[16,1536]{1,0:T(8,128)(2,1)S(1)}, bf16[16,1536]{1,0:T(8,128)(2,1)S(1)}, u32[]{:S(2)}, u32[]{:S(2)}) collective-permute-start(bf16[16,1536]{1,0:T(8,128)(2,1)S(1)} %get-tuple-element.16), channel_id=1, source_target_pairs={{16,0},{32,16},{48,32},{64,48},{80,64},{96,80},{112,96},{128,112},... | collective-permute-start | bytes 147464 | tf_op jit(solution)/shard_map/ppermute | solution.py:231
  154.6 7.4 %collective-permute-done.3.hi_ref = bf16[16,1536]{1,0:T(8,128)(2,1)S(1)} collective-permute-done((bf16[16,1536]{1,0:T(8,128)(2,1)S(1)}, bf16[16,1536]{1,0:T(8,128)(2,1)S(1)}, u32[]{:S(2)}, u32[]{:S(2)}) %collective-permute-start.3) | collective-permute-done | bytes 49184 | tf_op jit(solution)/shard_map/ppermute | solution.py:231
  161.9 3.3 %final.1 = (bf16[128,1024]{1,0:T(8,128)(2,1)}, bf16[128,1536]{1,0:T(8,128)(2,1)}) custom-call(s32[1]{0:T(128)S(6)} %copy.11.len_ref, s32[1]{0:T(128)} %bitcast.first_ref, bf16[16,128,256]{2,1,0:T(8,128)(2,1)S(1)} %all_to_all.11.in_ref, f32[128,1536]{1,0:T(8,128)S(1)} %get-tuple-element.14.gm_ref, bf16[16,1536]{1,0:T(8,128)(2,1)S(1)} %collective-permute-done.2.lo_ref, ...), custom_call_target="tpu_custom_call" | custom-call | tf_op jit(solution)/shard_map/final/pallas_call | solution.py:305
  165.2 0.7 convert_add_fusion
  (27 shorter events, 1.5 us)
Async XLA Ops:
  1.5 10.9 %collective-permute-start.1 = (bf16[16,1536]{1,0:T(8,128)(2,1)S(1)}, bf16[16,1536]{1,0:T(8,128)(2,1)S(1)}, u32[]{:S(2)}, u32[]{:S(2)}) collective-permute-start(bf16[16,1536]{1,0:T(8,128)(2,1)S(1)} %get-tuple-element.19), channel_id=1, source_target_pairs={{16,0},{32,16},{48,32},{64,48},{80,64},{96,80},{112,96},{128,112},... | collective-permute-start | bytes 147464 | tf_op jit(solution)/shard_map/ppermute | solution.py:231
  4.0 8.3 %collective-permute-start = (bf16[16,1536]{1,0:T(8,128)(2,1)S(1)}, bf16[16,1536]{1,0:T(8,128)(2,1)S(1)}, u32[]{:S(2)}, u32[]{:S(2)}) collective-permute-start(bf16[16,1536]{1,0:T(8,128)(2,1)S(1)} %get-tuple-element.20), channel_id=1, source_target_pairs={{0,16},{16,32},{32,48},{48,64},{64,80},{80,96},{96,112},{112,128},... | collective-permute-start | bytes 147464 | tf_op jit(solution)/shard_map/ppermute | solution.py:231
  12.3 1.9 %copy-start = (bf16[1536,1024]{1,0:T(8,128)(2,1)S(1)}, bf16[1536,1024]{1,0:T(8,128)(2,1)}, u32[]{:S(2)}) copy-start(bf16[1536,1024]{1,0:T(8,128)(2,1)} %wq_ref.3) | copy-start | bytes 9437188
  14.2 1.9 %copy-start.2 = (bf16[1536,1024]{1,0:T(8,128)(2,1)S(1)}, bf16[1536,1024]{1,0:T(8,128)(2,1)}, u32[]{:S(2)}) copy-start(bf16[1536,1024]{1,0:T(8,128)(2,1)} %wk_ref.3) | copy-start | bytes 9437188
  16.1 1.9 %copy-start.4 = (bf16[1536,1024]{1,0:T(8,128)(2,1)S(1)}, bf16[1536,1024]{1,0:T(8,128)(2,1)}, u32[]{:S(2)}) copy-start(bf16[1536,1024]{1,0:T(8,128)(2,1)} %wv_ref.3) | copy-start | bytes 9437188
  18.0 1.0 copy-start.6
  19.0 0.9 copy-start.8
  19.9 0.9 copy-start.10
  20.9 105.0 %copy-start.5 = (bf16[1536,1024]{1,0:T(8,128)(2,1)S(1)}, bf16[1536,1024]{1,0:T(8,128)(2,1)}, u32[]{:S(2)}) copy-start(bf16[1536,1024]{1,0:T(8,128)(2,1)} %wv_ref.3) | copy-start | bytes 9437188
  26.4 99.5 %copy-start.1 = (bf16[1536,1024]{1,0:T(8,128)(2,1)S(1)}, bf16[1536,1024]{1,0:T(8,128)(2,1)}, u32[]{:S(2)}) copy-start(bf16[1536,1024]{1,0:T(8,128)(2,1)} %wq_ref.3) | copy-start | bytes 9437188
  26.4 99.5 %copy-start.3 = (bf16[1536,1024]{1,0:T(8,128)(2,1)S(1)}, bf16[1536,1024]{1,0:T(8,128)(2,1)}, u32[]{:S(2)}) copy-start(bf16[1536,1024]{1,0:T(8,128)(2,1)} %wk_ref.3) | copy-start | bytes 9437188
  125.9 3.4 %copy-start.7 = (bf16[128,1536]{1,0:T(8,128)(2,1)S(1)}, bf16[128,1536]{1,0:T(8,128)(2,1)}, u32[]{:S(2)}) copy-start(bf16[128,1536]{1,0:T(8,128)(2,1)} %x_ref.3) | copy-start | bytes 1179652
  125.9 36.0 %copy-start.9 = (f32[31,1536]{1,0:T(8,128)S(1)}, f32[31,1536]{1,0:T(8,128)}, u32[]{:S(2)}) copy-start(f32[31,1536]{1,0:T(8,128)} %taps_ref.3) | copy-start | bytes 571396
  132.0 1.5 collective-permute-start.4
  133.5 4.1 %collective-permute-start.5 = (bf16[32,1536]{1,0:T(8,128)(2,1)S(1)}, bf16[32,1536]{1,0:T(8,128)(2,1)S(1)}, u32[]{:S(2)}, u32[]{:S(2)}) collective-permute-start(bf16[32,1536]{1,0:T(8,128)(2,1)S(1)} %add_convert_fusion.2), channel_id=1, source_target_pairs={{0,64},{16,80},{32,96},{48,112},{64,0},{80,16},{96,32},{112,48},{1... | collective-permute-start | bytes 294920 | tf_op jit(solution)/shard_map/ppermute | solution.py:304
  137.7 5.1 %collective-permute-start.6 = (bf16[32,1536]{1,0:T(8,128)(2,1)S(1)}, bf16[32,1536]{1,0:T(8,128)(2,1)S(1)}, u32[]{:S(2)}, u32[]{:S(2)}) collective-permute-start(bf16[32,1536]{1,0:T(8,128)(2,1)S(1)} %add_convert_fusion.1), channel_id=1, source_target_pairs={{0,128},{16,144},{32,160},{48,176},{64,192},{80,208},{96,224},{112... | collective-permute-start | bytes 294920 | tf_op jit(solution)/shard_map/ppermute | solution.py:304
  142.8 22.5 %collective-permute-start.7 = (bf16[32,1536]{1,0:T(8,128)(2,1)S(1)}, bf16[32,1536]{1,0:T(8,128)(2,1)S(1)}, u32[]{:S(2)}, u32[]{:S(2)}) collective-permute-start(bf16[32,1536]{1,0:T(8,128)(2,1)S(1)} %add_convert_fusion), channel_id=1, source_target_pairs={{0,32},{16,48},{32,0},{48,16},{64,96},{80,112},{96,64},{112,80},{1... | collective-permute-start | bytes 294920 | tf_op jit(solution)/shard_map/ppermute | solution.py:304
  142.9 11.7 %collective-permute-start.2 = (bf16[16,1536]{1,0:T(8,128)(2,1)S(1)}, bf16[16,1536]{1,0:T(8,128)(2,1)S(1)}, u32[]{:S(2)}, u32[]{:S(2)}) collective-permute-start(bf16[16,1536]{1,0:T(8,128)(2,1)S(1)} %get-tuple-element.15), channel_id=1, source_target_pairs={{0,16},{16,32},{32,48},{48,64},{64,80},{80,96},{96,112},{112,128},... | collective-permute-start | bytes 147464 | tf_op jit(solution)/shard_map/ppermute | solution.py:231
  152.6 9.3 %collective-permute-start.3 = (bf16[16,1536]{1,0:T(8,128)(2,1)S(1)}, bf16[16,1536]{1,0:T(8,128)(2,1)S(1)}, u32[]{:S(2)}, u32[]{:S(2)}) collective-permute-start(bf16[16,1536]{1,0:T(8,128)(2,1)S(1)} %get-tuple-element.16), channel_id=1, source_target_pairs={{16,0},{32,16},{48,32},{64,48},{80,64},{96,80},{112,96},{128,112},... | collective-permute-start | bytes 147464 | tf_op jit(solution)/shard_map/ppermute | solution.py:231

commit v2 on v1

v2 whole, which is shorter than its diff:
```python
import functools
import math

import jax
import jax.numpy as jnp
from jax import lax
from jax.experimental import pallas as pl
from jax.experimental.pallas import tpu as pltpu
from jax.sharding import PartitionSpec as P

HEADS = 16
HDIM = 64
KSIZE = 31
PAD = 16
LANES = 128
BF = jnp.bfloat16
F32 = jnp.float32
VMEM = pl.BlockSpec(memory_space=pltpu.VMEM)
SMEM = pl.BlockSpec(memory_space=pltpu.SMEM)
HBM = pl.BlockSpec(memory_space=pltpu.HBM)


def live_rows(first, rows, length):
    pos = first + lax.broadcasted_iota(jnp.int32, (rows, LANES), 0)
    return ((pos >= 0) & (pos < length)).astype(F32)


def ends(first, near_ref, far_ref, lanes, rows, length):
    odd = lax.rem(first // rows, 2) == 1
    near = near_ref[:, lanes].astype(F32)
    far = far_ref[:, lanes].astype(F32)
    low = jnp.where(odd, near, far) * live_rows(first - PAD, PAD, length)
    high = jnp.where(odd, far, near) * live_rows(first + rows, PAD, length)
    return low, high


def conv_chunk(padded, taps_ref, lanes, rows, reverse):
    total = None
    for r in range(8):
        acc = None
        for a in range(4):
            o = 8 * a + r
            if o == 0:
                continue
            j = KSIZE - o if reverse else o - 1
            term = taps_ref[j : j + 1, lanes] * padded[8 * a : 8 * a + rows + 8]
            acc = term if acc is None else acc + term
        part = acc[r : r + rows]
        total = part if total is None else total + part
    return total


def chunk(c):
    return pl.ds(pl.multiple_of(c * LANES, LANES), LANES)


def early_kernel(
    len_ref, first_ref, x_hbm, taps_hbm, g_hbm, wq_ref, wk_ref, wv_ref,
    conv_ref, w_ref, d_ref, x_ref, taps_ref, g_ref, sems,
):
    rows, width = x_ref.shape
    moves = ((x_hbm, x_ref), (taps_hbm, taps_ref), (g_hbm, g_ref))
    moves += tuple((w, w_ref.at[i]) for i, w in enumerate((wq_ref, wk_ref, wv_ref)))
    copies = [pltpu.make_async_copy(*m, sems.at[i]) for i, m in enumerate(moves)]
    for cp in copies:
        cp.start()
    live = live_rows(first_ref[0], rows, len_ref[0])
    zero = jnp.zeros((PAD, LANES), F32)
    for cp in copies[:3]:
        cp.wait()

    def conv_step(c, _):
        lanes = chunk(c)
        x = x_ref[:, lanes].astype(F32)
        padded = jnp.concatenate([zero, x * live, zero], axis=0)
        conv_ref[:, lanes] = x + conv_chunk(padded, taps_ref, lanes, rows, False)
        return 0

    lax.fori_loop(0, width // LANES, conv_step, 0)
    d_ref[...] = (g_ref[...].astype(F32) * live[:, 0:1]).T.astype(BF).reshape(d_ref.shape)
    for cp in copies[3:]:
        cp.wait()


def edge_convs(low, high, taps_ref, lanes, reverse):
    zero = jnp.zeros((2 * PAD, LANES), F32)
    top = conv_chunk(jnp.concatenate([low, zero], axis=0), taps_ref, lanes, PAD, reverse)
    end = conv_chunk(jnp.concatenate([zero, high], axis=0), taps_ref, lanes, PAD, reverse)
    return top, end


def pre_kernel(
    len_ref, first_ref, conv_ref, near_ref, far_ref, taps_ref, gain_ref, w_ref, d_ref,
    send_ref, mixed_ref, rstd_ref,
):
    rows, width = conv_ref.shape

    def conv_step(c, sq):
        lanes = chunk(c)
        low, high = ends(first_ref[0], near_ref, far_ref, lanes, rows, len_ref[0])
        top, end = edge_convs(low, high, taps_ref, lanes, False)
        mixed = jnp.concatenate(
            [
                conv_ref[:PAD, lanes] + top,
                conv_ref[PAD : rows - PAD, lanes],
                conv_ref[rows - PAD :, lanes] + end,
            ],
            axis=0,
        )
        mixed_ref[:, lanes] = mixed
        return sq + mixed * mixed

    sq = lax.fori_loop(0, width // LANES, conv_step, jnp.zeros((rows, LANES), F32))
    rstd = lax.rsqrt(jnp.sum(sq, axis=-1, keepdims=True) / width + 1e-05)
    rstd_ref[...] = jnp.broadcast_to(rstd, (rows, LANES))
    normed = (mixed_ref[...] * rstd * gain_ref[...]).astype(BF)
    for i in range(3):
        heads = jnp.dot(normed, w_ref[i], preferred_element_type=F32)
        send_ref[:, i * HDIM : (i + 1) * HDIM, :] = heads.T.astype(BF).reshape(HEADS, HDIM, rows)
    send_ref[:, 3 * HDIM :, :] = d_ref[...]


def attn_kernel(
    len_ref, in_ref, out_ref, qt_scr, dt_scr, kvt_scr, kv_scr, s_scr, e_scr, acc_scr,
    *, block, step,
):
    count, _, rows = in_ref.shape
    frames = count * rows
    length = len_ref[0]
    scale = HDIM ** (-0.5)
    factor = scale * math.log2(math.e)
    half = frames // 2
    for s in range(count):
        at = slice(s * rows, (s + 1) * rows)
        qt_scr[:, at] = in_ref[s, 0:HDIM, :]
        kvt = in_ref[s, HDIM : 3 * HDIM, :]
        kvt_scr[:, at] = kvt
        kv_scr[at, :] = kvt.T
        dt_scr[:, at] = in_ref[s, 3 * HDIM :, :]
    acc_scr[...] = jnp.zeros_like(acc_scr)
    steps = frames // step
    zero = jnp.zeros((HDIM, block), BF)

    def one_block(b, _):
        cols = pl.ds(pl.multiple_of(b * block, block), block)
        qt = jnp.concatenate([qt_scr[:, cols], zero], axis=0)
        q0 = qt.T
        top = None
        for i in range(steps):
            keys = slice(i * step, (i + 1) * step)
            s = jnp.dot(kv_scr[keys, :], qt, preferred_element_type=F32)
            if (i + 1) * step > half:
                pos = i * step + lax.broadcasted_iota(jnp.int32, (step, block), 0)
                s = jnp.where(pos < length, s, -1e30)
            s_scr[keys, :] = s
            part = jnp.max(s.reshape(step // 8, 8, block), axis=0)
            top = part if top is None else jnp.maximum(top, part)
        top = jnp.max(top, axis=0, keepdims=True)
        total = jnp.zeros((8, block), F32)
        out = jnp.zeros((HDIM, block), F32)
        for i in range(steps):
            keys = slice(i * step, (i + 1) * step)
            e = jnp.exp2((s_scr[keys, :] - top) * factor)
            s_scr[keys, :] = e
            eb = e.astype(BF)
            e_scr[keys, :] = eb
            total = total + jnp.sum(e.reshape(step // 8, 8, block), axis=0)
            out = out + jnp.dot(kvt_scr[HDIM:, keys], eb, preferred_element_type=F32)
        inv = 1.0 / jnp.sum(total, axis=0, keepdims=True)
        out = out * inv
        dt = dt_scr[:, cols].astype(F32) * inv
        delta = jnp.sum(dt * out, axis=0, keepdims=True)
        dt = jnp.concatenate([zero, dt.astype(BF)], axis=0)
        d0 = dt.T
        gq = jnp.zeros((HDIM, block), F32)
        for i in range(steps):
            keys = slice(i * step, (i + 1) * step)
            dp = jnp.dot(kv_scr[keys, :], dt, preferred_element_type=F32)
            ds = (s_scr[keys, :] * (dp - delta)).astype(BF)
            gq = gq + jnp.dot(kvt_scr[:HDIM, keys], ds, preferred_element_type=F32)
            acc_scr[keys, :] += jnp.dot(ds, q0, preferred_element_type=F32) + jnp.dot(
                e_scr[keys, :], d0, preferred_element_type=F32
            )
        gq = (gq * scale).astype(BF)
        out = out.astype(BF)
        for n in range(block // rows):
            at = slice(n * rows, (n + 1) * rows)
            src = b * (block // rows) + n
            out_ref[src, 0:HDIM, :] = gq[:, at]
            out_ref[src, 3 * HDIM : 4 * HDIM, :] = out[:, at]
        return 0

    lax.fori_loop(0, frames // block, one_block, 0)
    row = lax.broadcasted_iota(jnp.int32, (2 * HDIM, rows), 0)
    fix = jnp.where(row < HDIM, scale, 1.0)
    for s in range(count):
        acc = acc_scr[s * rows : (s + 1) * rows, :]
        out_ref[s, HDIM : 3 * HDIM, :] = (acc.T * fix).astype(BF)


def back_kernel(
    in_ref, wq_ref, wk_ref, wv_ref, mixed_ref, rstd_ref, gain_ref, gm_ref
):
    rows, width = mixed_ref.shape
    nt = (((1,), (1,)), ((), ()))
    grad = None
    for i, w_ref in enumerate((wq_ref, wk_ref, wv_ref)):
        feats = in_ref[:, i * HDIM : (i + 1) * HDIM, :].reshape(HEADS * HDIM, rows).T
        part = lax.dot_general(feats, w_ref[...], nt, preferred_element_type=F32)
        grad = part if grad is None else grad + part
    scaled = grad * gain_ref[...]
    mixed = mixed_ref[...]
    rstd = rstd_ref[:, 0:1]
    mean = jnp.sum(scaled * mixed, axis=-1, keepdims=True) / width
    gm = rstd * scaled - mixed * (rstd * rstd * rstd * mean)
    gm_ref[...] = gm


def taps_kernel(len_ref, first_ref, x_ref, near_ref, far_ref, gm_ref, out_ref):
    rows, width = x_ref.shape
    first = first_ref[0]
    odd = lax.rem(first // rows, 2) == 1
    live = live_rows(first, rows, len_ref[0])

    def step(c, _):
        lanes = chunk(c)
        low, high = ends(first, near_ref, far_ref, lanes, rows, len_ref[0])
        padded = jnp.concatenate([low, x_ref[:, lanes].astype(F32) * live, high], axis=0)
        gm = gm_ref[:, lanes]
        result = [None] * (KSIZE + 1)
        for r in range(8):
            fill = [jnp.zeros((r, LANES), F32)] if r else []
            ext = jnp.concatenate(fill + [gm, jnp.zeros((8 - r, LANES), F32)], axis=0)
            for a in range(4):
                o = 8 * a + r
                if o == 0:
                    continue
                prod = ext * padded[8 * a : 8 * a + rows + 8]
                result[o - 1] = jnp.sum(prod, axis=0, keepdims=True)
        result[KSIZE] = jnp.zeros((1, LANES), F32)
        out_ref[: KSIZE + 1, lanes] = jnp.concatenate(result, axis=0).astype(BF)
        head = gm[:PAD]
        tail = gm[rows - PAD :]
        out_ref[KSIZE + 1 : KSIZE + 1 + PAD, lanes] = jnp.where(odd, head, tail).astype(BF)
        out_ref[KSIZE + 1 + PAD :, lanes] = jnp.where(odd, tail, head).astype(BF)
        return 0

    lax.fori_loop(0, width // LANES, step, 0)


def own_kernel(len_ref, first_ref, in_ref, gm_ref, taps_ref, attn_ref, own_ref):
    rows, width = gm_ref.shape
    live = live_rows(first_ref[0], rows, len_ref[0])
    zero = jnp.zeros((PAD, LANES), F32)

    def step(c, _):
        lanes = chunk(c)
        gm = gm_ref[:, lanes]
        padded = jnp.concatenate([zero, gm, zero], axis=0)
        own_ref[:, lanes] = gm + live * conv_chunk(padded, taps_ref, lanes, rows, True)
        return 0

    lax.fori_loop(0, width // LANES, step, 0)
    out = in_ref[:, 3 * HDIM : 4 * HDIM, :].reshape(HEADS * HDIM, rows).T
    attn_ref[...] = (out.astype(F32) * live[:, 0:1]).astype(BF)


def final_kernel(
    len_ref, first_ref, own_ref, near_ref, far_ref, taps_ref, mine_ref, gi_ref, gk_ref,
    *, frames,
):
    rows, width = own_ref.shape
    first = first_ref[0]
    live = live_rows(first, rows, len_ref[0])
    near_edge = near_ref.at[KSIZE + 1 : KSIZE + 1 + PAD]
    far_edge = far_ref.at[KSIZE + 1 :]

    def step(c, _):
        lanes = chunk(c)
        low, high = ends(first, near_edge, far_edge, lanes, rows, frames)
        top, end = edge_convs(low, high, taps_ref, lanes, True)
        gi_ref[:PAD, lanes] = (own_ref[:PAD, lanes] + live[:PAD] * top).astype(BF)
        gi_ref[PAD : rows - PAD, lanes] = own_ref[PAD : rows - PAD, lanes].astype(BF)
        gi_ref[rows - PAD :, lanes] = (
            own_ref[rows - PAD :, lanes] + live[rows - PAD :] * end
        ).astype(BF)
        gk_ref[:, lanes] = mine_ref[:KSIZE, lanes].astype(F32) + far_ref[:KSIZE, lanes].astype(F32)
        return 0

    lax.fori_loop(0, width // LANES, step, 0)


def params(mib):
    return pltpu.CompilerParams(vmem_limit_bytes=mib << 20)


def cost(us):
    return pl.CostEstimate(flops=int(us * 1.1e9), bytes_accessed=1024, transcendentals=0)


def local(inputs, lengths, kernel, gain, q_weight, k_weight, v_weight, grad_attn):
    rows, width = inputs.shape
    count = lax.axis_size("seq")
    frames = rows * count
    feats = HEADS * HDIM
    sds = jax.ShapeDtypeStruct
    here = lax.axis_index("seq")
    odd = lax.rem(here, 2)
    first = (here * rows).astype(jnp.int32).reshape(1)
    gain = gain.reshape(1, width)

    def peer(mine, move):
        return lax.ppermute(mine, "seq", [(i, move(i)) for i in range(count)])

    def near(mine):
        return peer(mine, lambda i: i ^ 1)

    def far(mine):
        return peer(mine, lambda i: (i + 1 if i % 2 else i - 1) % count)

    a2a = functools.partial(
        lax.all_to_all, axis_name="seq", split_axis=0, concat_axis=0, tiled=True
    )
    x_far = far(lax.dynamic_slice_in_dim(inputs, odd * (rows - PAD), PAD))
    x_near = near(lax.dynamic_slice_in_dim(inputs, (1 - odd) * (rows - PAD), PAD))

    def in_hbm(array):
        return pltpu.with_memory_space_constraint(array, pltpu.HBM)

    own, weights, douts = pl.pallas_call(
        early_kernel,
        name="early",
        out_shape=(
            pltpu.VMEM((rows, width), F32),
            pltpu.VMEM((3, width, feats), BF),
            pltpu.VMEM((HEADS, HDIM, rows), BF),
        ),
        in_specs=[SMEM, SMEM] + [HBM] * 6,
        out_specs=(VMEM,) * 3,
        scratch_shapes=[
            pltpu.VMEM((rows, width), BF),
            pltpu.VMEM((KSIZE, width), F32),
            pltpu.VMEM((rows, feats), BF),
            pltpu.SemaphoreType.DMA((6,)),
        ],
        compiler_params=params(16),
        cost_estimate=cost(6),
    )(lengths, first, *(in_hbm(a) for a in (inputs, kernel, grad_attn, q_weight, k_weight, v_weight)))
    send, mixed, rstd = pl.pallas_call(
        pre_kernel,
        name="pre",
        out_shape=(
            sds((HEADS, 4 * HDIM, rows), BF),
            sds((rows, width), F32),
            sds((rows, LANES), F32),
        ),
        in_specs=[SMEM, SMEM] + [VMEM] * 7,
        out_specs=(VMEM,) * 3,
        compiler_params=params(16),
        cost_estimate=cost(3),
    )(lengths, first, own, x_near, x_far, kernel, gain, weights, douts)

    block, step = 512, 1024
    heads_out = pl.pallas_call(
        functools.partial(attn_kernel, block=block, step=step),
        name="attn",
        out_shape=sds((HEADS, 4 * HDIM, rows), BF),
        in_specs=[SMEM, VMEM],
        out_specs=VMEM,
        scratch_shapes=[
            pltpu.VMEM((HDIM, frames), BF),
            pltpu.VMEM((HDIM, frames), BF),
            pltpu.VMEM((2 * HDIM, frames), BF),
            pltpu.VMEM((frames, 2 * HDIM), BF),
            pltpu.VMEM((frames, block), F32),
            pltpu.VMEM((frames, block), BF),
            pltpu.VMEM((frames, 2 * HDIM), F32),
        ],
        compiler_params=params(32),
        cost_estimate=cost(17),
    )(lengths, a2a(send))
    grads = a2a(heads_out)

    gm = pl.pallas_call(
        back_kernel,
        name="back",
        out_shape=sds((rows, width), F32),
        in_specs=[VMEM] * 7,
        out_specs=VMEM,
        compiler_params=params(16),
        cost_estimate=cost(4),
    )(grads, q_weight, k_weight, v_weight, mixed, rstd, gain)
    taps = pl.pallas_call(
        taps_kernel,
        name="taps",
        out_shape=sds((KSIZE + 1 + 2 * PAD, width), BF),
        in_specs=[SMEM, SMEM] + [VMEM] * 4,
        out_specs=VMEM,
        compiler_params=params(16),
        cost_estimate=cost(3),
    )(lengths, first, inputs, x_near, x_far, gm)

    got = near(taps[: KSIZE + 1 + PAD])
    total = taps[: KSIZE + 1].astype(F32) + got[: KSIZE + 1].astype(F32)
    for bit in (4, 8):
        mine = total.astype(BF)
        total = mine.astype(F32) + peer(mine, lambda i: i ^ bit).astype(F32)
    mine = jnp.concatenate([total.astype(BF), taps[KSIZE + 1 + PAD :]], axis=0)
    last = far(mine)
    attn, own_gi = pl.pallas_call(
        own_kernel,
        name="own",
        out_shape=(sds((rows, feats), BF), sds((rows, width), F32)),
        in_specs=[SMEM, SMEM] + [VMEM] * 3,
        out_specs=(VMEM,) * 2,
        compiler_params=params(16),
        cost_estimate=cost(3),
    )(lengths, first, grads, gm, kernel)
    grad_input, grad_kernel = pl.pallas_call(
        functools.partial(final_kernel, frames=frames),
        name="final",
        out_shape=(sds((rows, width), BF), sds((KSIZE, width), F32)),
        in_specs=[SMEM, SMEM] + [VMEM] * 5,
        out_specs=(VMEM,) * 2,
        compiler_params=params(16),
        cost_estimate=cost(1),
    )(lengths, first, own_gi, got, last, kernel, mine)
    return (attn, grad_input, grad_kernel)


def solution(mesh):
    placed = (P(("dp", "seq"), None), P("dp"), P(), P(), P(), P(), P(), P(("dp", "seq"), None))
    return jax.shard_map(
        local,
        mesh=mesh,
        in_specs=placed,
        out_specs=(P(("dp", "seq"), None), P(("dp", "seq"), None), P("dp", None)),
        check_vma=False,
    )
```

time: 167 us -> 136 us (0.81)
  the two profiles are of different devices: /device:TPU:71 before, /device:TPU:34 now
where the time goes in v2:
time: 136 us
  blocking collectives  70 us (51%)
  Pallas kernels  33.6 us (25%)
  waiting for transfers between devices  20.1 us (15%)
  starting transfers between devices  9.53 us (7%)
  between operations  1.45 us (1%)
    all_to_all x1, blocking collectives, local(): a2a(send)  37.8 us
    all_to_all x1, blocking collectives, local(): grads = a2a(heads_out)  32.2 us
    ppermute x6, waiting for transfers between devices, peer(): return lax.ppermute(mine, 'seq', [(i, move(i)) for i in range(count)])  20.1 us
    pallas_call x1, Pallas kernels, local(): pl.pallas_call(functools.partial(attn_kernel, block=block, step=step), na...  16.3 us
    ppermute x6, starting transfers between devices, peer(): return lax.ppermute(mine, 'seq', [(i, move(i)) for i in range(count)])  9.53 us
    pallas_call x1, Pallas kernels, local(): pl.pallas_call(early_kernel, name='early', out_shape=(pltpu.VMEM((rows, w...  4.14 us
    pallas_call x1, Pallas kernels, local(): pl.pallas_call(back_kernel, name='back', out_shape=sds((rows, width), F32...  3.4 us
    pallas_call x1, Pallas kernels, local(): pl.pallas_call(own_kernel, name='own', out_shape=(sds((rows, feats), BF),...  3.1 us
  transfers between devices with their start and end apart: 6, of which 4 were waited for; matrix products, arithmetic and copies ran while one was open for 0% of the time, Pallas kernels for 5%

profile of v2, /device:TPU:34, one launch (start us, length us, event | category | flops | bytes accessed | tf_op | source)
XLA Modules:
  0.0 135.6 jit_solution(437933816934866021)
XLA Ops:
  0.6 0.8 constant_dynamic-slice_fusion
  1.5 8.2 %collective-permute-start.1 = (bf16[16,1536]{1,0:T(8,128)(2,1)S(1)}, bf16[16,1536]{1,0:T(8,128)(2,1)S(1)}, u32[]{:S(2)}, u32[]{:S(2)}) collective-permute-start(bf16[16,1536]{1,0:T(8,128)(2,1)S(1)} %get-tuple-element.23), channel_id=1, source_target_pairs={{0,240},{16,32},{32,16},{48,64},{64,48},{80,96},{96,80},{112,128},... | collective-permute-start | bytes 147464 | tf_op jit(solution)/shard_map/ppermute | solution.py:313
  9.7 0.0 collective-permute-start
  10.4 0.0 copy-start.5
  10.4 0.0 copy-start.4
  10.4 4.1 %early.1 = (f32[128,1536]{1,0:T(8,128)S(1)}, bf16[3,1536,1024]{2,1,0:T(8,128)(2,1)S(1)}, bf16[16,64,128]{2,1,0:T(8,128)(2,1)S(1)}) custom-call(s32[1]{0:T(128)S(6)} %copy.11.len_ref, s32[1]{0:T(128)} %bitcast.first_ref, bf16[128,1536]{1,0:T(8,128)(2,1)} %x_ref.1, f32[31,1536]{1,0:T(8,128)} %taps_ref.5, bf16[128,1024]{1,0:T(8,128)(2,1)} %g_hbm.1, ...), custom_call_target="tpu_custom_call" | custom-call | flops 6600000000 | bytes 1024 | tf_op jit(solution)/shard_map/early/pallas_call | solution.py:330
  14.6 0.0 collective-permute-done.near_ref
  14.6 2.4 %pre.1 = (bf16[16,256,128]{2,1,0:T(8,128)(2,1)S(1)}, f32[128,1536]{1,0:T(8,128)S(1)}, f32[128,128]{1,0:T(8,128)S(1)}) custom-call(s32[1]{0:T(128)S(6)} %copy.11.len_ref, s32[1]{0:T(128)} %bitcast.first_ref, f32[128,1536]{1,0:T(8,128)S(1)} %get-tuple-element.13.conv_ref, bf16[16,1536]{1,0:T(8,128)(2,1)S(1)} %collective-permute-done.near_ref, ...), custom_call_target="tpu_custom_call" | custom-call | flops 3300000000 | bytes 1024 | tf_op jit(solution)/shard_map/pre/pallas_call | solution.py:349
  17.0 37.8 %all_to_all.10.in_ref = bf16[16,256,128]{2,1,0:T(8,128)(2,1)S(1)} all-to-all(bf16[16,256,128]{2,1,0:T(8,128)(2,1)S(1)} %get-tuple-element.16), channel_id=1, replica_groups=mesh['seq'=16,'dp'=16] {'seq'}, dimensions={0} | all-to-all | bytes 2097152 | tf_op jit(solution)/shard_map/all_to_all | solution.py:381
  54.8 16.3 %attn.1 = bf16[16,256,128]{2,1,0:T(8,128)(2,1)S(1)} custom-call(s32[1]{0:T(128)S(6)} %copy.11.len_ref, bf16[16,256,128]{2,1,0:T(8,128)(2,1)S(1)} %all_to_all.10.in_ref), custom_call_target="tpu_custom_call" | custom-call | flops 18699999232 | bytes 1024 | tf_op jit(solution)/shard_map/attn/pallas_call | solution.py:364
  71.2 32.2 %all_to_all.11.in_ref = bf16[16,256,128]{2,1,0:T(8,128)(2,1)S(1)} all-to-all(bf16[16,256,128]{2,1,0:T(8,128)(2,1)S(1)} %attn.1), channel_id=1, replica_groups=mesh['seq'=16,'dp'=16] {'seq'}, dimensions={0} | all-to-all | bytes 2097152 | tf_op jit(solution)/shard_map/all_to_all | solution.py:382
  103.4 0.0 copy-start
  103.4 3.4 %back.1.gm_ref = f32[128,1536]{1,0:T(8,128)S(1)} custom-call(bf16[16,256,128]{2,1,0:T(8,128)(2,1)S(1)} %all_to_all.11.in_ref, bf16[1536,1024]{1,0:T(8,128)(2,1)S(1)} %copy-done.1, bf16[1536,1024]{1,0:T(8,128)(2,1)S(1)} %copy-done.2, bf16[1536,1024]{1,0:T(8,128)(2,1)S(1)} %copy-done.3, f32[128,1536]{1,0:T(8,128)S(1)} %get-tuple-element.17.mixed_ref, ...), custom_call_target="tpu_custom_call" | custom-call | flops 4400000000 | bytes 1024 | tf_op jit(solution)/shard_map/back/pallas_call | solution.py:384
  106.8 2.7 %taps.1 = bf16[64,1536]{1,0:T(8,128)(2,1)S(1)} custom-call(s32[1]{0:T(128)S(6)} %copy.11.len_ref, s32[1]{0:T(128)} %bitcast.first_ref, bf16[128,1536]{1,0:T(8,128)(2,1)S(1)} %copy-done, bf16[16,1536]{1,0:T(8,128)(2,1)S(1)} %collective-permute-done.near_ref, bf16[16,1536]{1,0:T(8,128)(2,1)S(1)} %collective-permute-done.1.far_ref, f32[128,1536]{1,0:T(8,128)S(1)} %back.1.gm_ref), custom_call_target="tpu_custom_call" | custom-call | flops 3300000000 | bytes 1024 | tf_op jit(solution)/shard_map/taps/pallas_call | solution.py:393
  109.5 0.1 collective-permute-start.2
  109.6 1.3 collective-permute-done.2.near_ref
  111.0 0.1 collective-permute-start.3
  111.1 4.8 %collective-permute-done.3 = bf16[32,1536]{1,0:T(8,128)(2,1)S(1)} collective-permute-done((bf16[32,1536]{1,0:T(8,128)(2,1)S(1)}, bf16[32,1536]{1,0:T(8,128)(2,1)S(1)}, u32[]{:S(2)}, u32[]{:S(2)}) %collective-permute-start.3) | collective-permute-done | bytes 98336 | tf_op jit(solution)/shard_map/ppermute | solution.py:313
  115.9 0.9 collective-permute-start.4
  116.9 5.3 %collective-permute-done.4 = bf16[32,1536]{1,0:T(8,128)(2,1)S(1)} collective-permute-done((bf16[32,1536]{1,0:T(8,128)(2,1)S(1)}, bf16[32,1536]{1,0:T(8,128)(2,1)S(1)}, u32[]{:S(2)}, u32[]{:S(2)}) %collective-permute-start.4) | collective-permute-done | bytes 98336 | tf_op jit(solution)/shard_map/ppermute | solution.py:313
  122.2 0.1 collective-permute-start.5
  122.3 3.1 %own.1 = (bf16[128,1024]{1,0:T(8,128)(2,1)}, f32[128,1536]{1,0:T(8,128)S(1)}) custom-call(s32[1]{0:T(128)S(6)} %copy.11.len_ref, s32[1]{0:T(128)} %bitcast.first_ref, bf16[16,256,128]{2,1,0:T(8,128)(2,1)S(1)} %all_to_all.11.in_ref, f32[128,1536]{1,0:T(8,128)S(1)} %back.1.gm_ref, f32[31,1536]{1,0:T(8,128)S(1)} %copy-done.4), custom_call_target="tpu_custom_call" | custom-call | flops 3300000000 | bytes 1024 | tf_op jit(solution)/shard_map/own/pallas_call | solution.py:410
  125.4 8.7 %collective-permute-done.5.far_ref = bf16[48,1536]{1,0:T(8,128)(2,1)S(1)} collective-permute-done((bf16[48,1536]{1,0:T(8,128)(2,1)S(1)}, bf16[48,1536]{1,0:T(8,128)(2,1)S(1)}, u32[]{:S(2)}, u32[]{:S(2)}) %collective-permute-start.5) | collective-permute-done | bytes 147488 | tf_op jit(solution)/shard_map/ppermute | solution.py:313
  134.1 1.6 %final.1 = (bf16[128,1536]{1,0:T(8,128)(2,1)}, f32[31,1536]{1,0:T(8,128)}) custom-call(s32[1]{0:T(128)S(6)} %copy.11.len_ref, s32[1]{0:T(128)} %bitcast.first_ref, f32[128,1536]{1,0:T(8,128)S(1)} %get-tuple-element.20.own_ref, bf16[48,1536]{1,0:T(8,128)(2,1)S(1)} %collective-permute-done.2.near_ref, bf16[48,1536]{1,0:T(8,128)(2,1)S(1)} %collective-permute-done.5.far_ref, ...), custom_call_target="tpu_custom_call" | custom-call | flops 1100000000 | bytes 1024 | tf_op jit(solution)/shard_map/final/pallas_call | solution.py:419
  (17 shorter events, 0.1 us)
Async XLA Ops:
  1.5 13.1 %collective-permute-start.1 = (bf16[16,1536]{1,0:T(8,128)(2,1)S(1)}, bf16[16,1536]{1,0:T(8,128)(2,1)S(1)}, u32[]{:S(2)}, u32[]{:S(2)}) collective-permute-start(bf16[16,1536]{1,0:T(8,128)(2,1)S(1)} %get-tuple-element.23), channel_id=1, source_target_pairs={{0,240},{16,32},{32,16},{48,64},{64,48},{80,96},{96,80},{112,128},... | collective-permute-start | bytes 147464 | tf_op jit(solution)/shard_map/ppermute | solution.py:313
  9.7 4.9 %collective-permute-start = (bf16[16,1536]{1,0:T(8,128)(2,1)S(1)}, bf16[16,1536]{1,0:T(8,128)(2,1)S(1)}, u32[]{:S(2)}, u32[]{:S(2)}) collective-permute-start(bf16[16,1536]{1,0:T(8,128)(2,1)S(1)} %get-tuple-element.24), channel_id=1, source_target_pairs={{0,16},{16,0},{32,48},{48,32},{64,80},{80,64},{96,112},{112,96},{1... | collective-permute-start | bytes 147464 | tf_op jit(solution)/shard_map/ppermute | solution.py:313
  10.4 4.2 %copy-start.5 = (f32[1536]{0:T(1024)S(1)}, f32[1536]{0:T(1024)}, u32[]{:S(2)}) copy-start(f32[1536]{0:T(1024)} %param.11) | copy-start | bytes 18436
  10.4 4.2 %copy-start.4 = (f32[31,1536]{1,0:T(8,128)S(1)}, f32[31,1536]{1,0:T(8,128)}, u32[]{:S(2)}) copy-start(f32[31,1536]{1,0:T(8,128)} %taps_ref.5) | copy-start | bytes 571396
  54.8 48.5 %copy-start.1 = (bf16[1536,1024]{1,0:T(8,128)(2,1)S(1)}, bf16[1536,1024]{1,0:T(8,128)(2,1)}, u32[]{:S(2)}) copy-start(bf16[1536,1024]{1,0:T(8,128)(2,1)} %wq_ref.3) | copy-start | bytes 9437188
  54.8 48.5 %copy-start.2 = (bf16[1536,1024]{1,0:T(8,128)(2,1)S(1)}, bf16[1536,1024]{1,0:T(8,128)(2,1)}, u32[]{:S(2)}) copy-start(bf16[1536,1024]{1,0:T(8,128)(2,1)} %wk_ref.3) | copy-start | bytes 9437188
  54.8 48.5 %copy-start.3 = (bf16[1536,1024]{1,0:T(8,128)(2,1)S(1)}, bf16[1536,1024]{1,0:T(8,128)(2,1)}, u32[]{:S(2)}) copy-start(bf16[1536,1024]{1,0:T(8,128)(2,1)} %wv_ref.3) | copy-start | bytes 9437188
  103.4 3.4 %copy-start = (bf16[128,1536]{1,0:T(8,128)(2,1)S(1)}, bf16[128,1536]{1,0:T(8,128)(2,1)}, u32[]{:S(2)}) copy-start(bf16[128,1536]{1,0:T(8,128)(2,1)} %x_ref.1) | copy-start | bytes 1179652
  109.5 1.5 %collective-permute-start.2 = (bf16[48,1536]{1,0:T(8,128)(2,1)S(1)}, bf16[48,1536]{1,0:T(8,128)(2,1)S(1)}, u32[]{:S(2)}, u32[]{:S(2)}) collective-permute-start(bf16[48,1536]{1,0:T(8,128)(2,1)S(1)} %slice.16), channel_id=1, source_target_pairs={{0,16},{16,0},{32,48},{48,32},{64,80},{80,64},{96,112},{112,96},{1... | collective-permute-start | bytes 442376 | tf_op jit(solution)/shard_map/ppermute | solution.py:313
  111.0 4.9 %collective-permute-start.3 = (bf16[32,1536]{1,0:T(8,128)(2,1)S(1)}, bf16[32,1536]{1,0:T(8,128)(2,1)S(1)}, u32[]{:S(2)}, u32[]{:S(2)}) collective-permute-start(bf16[32,1536]{1,0:T(8,128)(2,1)S(1)} %add_convert_fusion.2), channel_id=1, source_target_pairs={{0,64},{16,80},{32,96},{48,112},{64,0},{80,16},{96,32},{112,48},{1... | collective-permute-start | bytes 294920 | tf_op jit(solution)/shard_map/ppermute | solution.py:313
  115.9 6.2 %collective-permute-start.4 = (bf16[32,1536]{1,0:T(8,128)(2,1)S(1)}, bf16[32,1536]{1,0:T(8,128)(2,1)S(1)}, u32[]{:S(2)}, u32[]{:S(2)}) collective-permute-start(bf16[32,1536]{1,0:T(8,128)(2,1)S(1)} %add_convert_fusion.1), channel_id=1, source_target_pairs={{0,128},{16,144},{32,160},{48,176},{64,192},{80,208},{96,224},{112... | collective-permute-start | bytes 294920 | tf_op jit(solution)/shard_map/ppermute | solution.py:313
  122.2 11.9 %collective-permute-start.5 = (bf16[48,1536]{1,0:T(8,128)(2,1)S(1)}, bf16[48,1536]{1,0:T(8,128)(2,1)S(1)}, u32[]{:S(2)}, u32[]{:S(2)}) collective-permute-start(bf16[48,1536]{1,0:T(8,128)(2,1)S(1)} %pad_maximum_fusion.mine_ref), channel_id=1, source_target_pairs={{0,240},{16,32},{32,16},{48,64},{64,48},{80,96},{96,80},{112,128},... | collective-permute-start | bytes 442376 | tf_op jit(solution)/shard_map/ppermute | solution.py:313

commit v3 on v2

--- a/solution.py
+++ b/solution.py
@@ -122,7 +122,7 @@
 
 def attn_kernel(
     len_ref, in_ref, out_ref, qt_scr, dt_scr, kvt_scr, kv_scr, s_scr, e_scr, acc_scr,
-    *, block, step,
+    *, block, sstep, step,
 ):
     count, _, rows = in_ref.shape
     frames = count * rows
@@ -130,6 +130,8 @@
     scale = HDIM ** (-0.5)
     factor = scale * math.log2(math.e)
     half = frames // 2
+    steps = frames // step
+    blocks = frames // block
     for s in range(count):
         at = slice(s * rows, (s + 1) * rows)
         qt_scr[:, at] = in_ref[s, 0:HDIM, :]
@@ -138,59 +140,74 @@
         kv_scr[at, :] = kvt.T
         dt_scr[:, at] = in_ref[s, 3 * HDIM :, :]
     acc_scr[...] = jnp.zeros_like(acc_scr)
-    steps = frames // step
     zero = jnp.zeros((HDIM, block), BF)
-
-    def one_block(b, _):
-        cols = pl.ds(pl.multiple_of(b * block, block), block)
-        qt = jnp.concatenate([qt_scr[:, cols], zero], axis=0)
-        q0 = qt.T
+    none = jnp.zeros((HDIM, block), F32)
+
+    def query(b):
+        return jnp.concatenate([qt_scr[:, b * block : (b + 1) * block], zero], axis=0)
+
+    def scores(b):
+        qt = query(b)
         top = None
-        for i in range(steps):
-            keys = slice(i * step, (i + 1) * step)
+        for i in range(frames // sstep):
+            keys = slice(i * sstep, (i + 1) * sstep)
             s = jnp.dot(kv_scr[keys, :], qt, preferred_element_type=F32)
-            if (i + 1) * step > half:
-                pos = i * step + lax.broadcasted_iota(jnp.int32, (step, block), 0)
+            if (i + 1) * sstep > half:
+                pos = i * sstep + lax.broadcasted_iota(jnp.int32, (sstep, block), 0)
                 s = jnp.where(pos < length, s, -1e30)
-            s_scr[keys, :] = s
-            part = jnp.max(s.reshape(step // 8, 8, block), axis=0)
+            s_scr[b % 2, keys, :] = s
+            part = jnp.max(s.reshape(sstep // 8, 8, block), axis=0)
             top = part if top is None else jnp.maximum(top, part)
-        top = jnp.max(top, axis=0, keepdims=True)
-        total = jnp.zeros((8, block), F32)
-        out = jnp.zeros((HDIM, block), F32)
-        for i in range(steps):
-            keys = slice(i * step, (i + 1) * step)
-            e = jnp.exp2((s_scr[keys, :] - top) * factor)
-            s_scr[keys, :] = e
-            eb = e.astype(BF)
-            e_scr[keys, :] = eb
-            total = total + jnp.sum(e.reshape(step // 8, 8, block), axis=0)
-            out = out + jnp.dot(kvt_scr[HDIM:, keys], eb, preferred_element_type=F32)
+        return jnp.max(top, axis=0, keepdims=True)
+
+    def forward(b, i, top, total, out):
+        keys = slice(i * step, (i + 1) * step)
+        e = jnp.exp2((s_scr[b % 2, keys, :] - top) * factor)
+        s_scr[b % 2, keys, :] = e
+        eb = e.astype(BF)
+        e_scr[b % 2, keys, :] = eb
+        total = total + jnp.sum(e.reshape(step // 8, 8, block), axis=0)
+        return total, out + jnp.dot(kvt_scr[HDIM:, keys], eb, preferred_element_type=F32)
+
+    def between(b, total, out):
         inv = 1.0 / jnp.sum(total, axis=0, keepdims=True)
         out = out * inv
-        dt = dt_scr[:, cols].astype(F32) * inv
+        dt = dt_scr[:, b * block : (b + 1) * block].astype(F32) * inv
         delta = jnp.sum(dt * out, axis=0, keepdims=True)
-        dt = jnp.concatenate([zero, dt.astype(BF)], axis=0)
-        d0 = dt.T
-        gq = jnp.zeros((HDIM, block), F32)
+        return out, delta, jnp.concatenate([zero, dt.astype(BF)], axis=0)
+
+    def backward(b, i, q0, d0, dt, delta, gq):
+        keys = slice(i * step, (i + 1) * step)
+        dp = jnp.dot(kv_scr[keys, :], dt, preferred_element_type=F32)
+        ds = (s_scr[b % 2, keys, :] * (dp - delta)).astype(BF)
+        acc_scr[keys, :] += jnp.dot(ds, q0, preferred_element_type=F32) + jnp.dot(
+            e_scr[b % 2, keys, :], d0, preferred_element_type=F32
+        )
+        return gq + jnp.dot(kvt_scr[:HDIM, keys], ds, preferred_element_type=F32)
+
+    state = None
+    for b in range(blocks + 1):
+        total, ahead, gq = jnp.zeros((8, block), F32), none, none
+        if b < blocks:
+            top = scores(b)
+        if b > 0:
+            out, delta, dt = state
+            q0, d0 = query(b - 1).T, dt.T
         for i in range(steps):
-            keys = slice(i * step, (i + 1) * step)
-            dp = jnp.dot(kv_scr[keys, :], dt, preferred_element_type=F32)
-            ds = (s_scr[keys, :] * (dp - delta)).astype(BF)
-            gq = gq + jnp.dot(kvt_scr[:HDIM, keys], ds, preferred_element_type=F32)
-            acc_scr[keys, :] += jnp.dot(ds, q0, preferred_element_type=F32) + jnp.dot(
-                e_scr[keys, :], d0, preferred_element_type=F32
-            )
-        gq = (gq * scale).astype(BF)
-        out = out.astype(BF)
-        for n in range(block // rows):
-            at = slice(n * rows, (n + 1) * rows)
-            src = b * (block // rows) + n
-            out_ref[src, 0:HDIM, :] = gq[:, at]
-            out_ref[src, 3 * HDIM : 4 * HDIM, :] = out[:, at]
-        return 0
-
-    lax.fori_loop(0, frames // block, one_block, 0)
+            if b < blocks:
+                total, ahead = forward(b, i, top, total, ahead)
+            if b > 0:
+                gq = backward(b - 1, i, q0, d0, dt, delta, gq)
+        if b < blocks:
+            state = between(b, total, ahead)
+        if b > 0:
+            gq = (gq * scale).astype(BF)
+            out = out.astype(BF)
+            for n in range(block // rows):
+                at = slice(n * rows, (n + 1) * rows)
+                dest = (b - 1) * (block // rows) + n
+                out_ref[dest, 0:HDIM, :] = gq[:, at]
+                out_ref[dest, 3 * HDIM : 4 * HDIM, :] = out[:, at]
     row = lax.broadcasted_iota(jnp.int32, (2 * HDIM, rows), 0)
     fix = jnp.where(row < HDIM, scale, 1.0)
     for s in range(count):
@@ -216,14 +233,16 @@
     gm_ref[...] = gm
 
 
-def taps_kernel(len_ref, first_ref, x_ref, near_ref, far_ref, gm_ref, out_ref):
+def taps_kernel(
+    len_ref, first_ref, half_ref, x_ref, near_ref, far_ref, gm_ref, keep_ref, give_ref, edge_ref
+):
     rows, width = x_ref.shape
     first = first_ref[0]
     odd = lax.rem(first // rows, 2) == 1
     live = live_rows(first, rows, len_ref[0])
-
-    def step(c, _):
-        lanes = chunk(c)
+    count = width // 2 // LANES
+
+    def terms(lanes):
         low, high = ends(first, near_ref, far_ref, lanes, rows, len_ref[0])
         padded = jnp.concatenate([low, x_ref[:, lanes].astype(F32) * live, high], axis=0)
         gm = gm_ref[:, lanes]
@@ -238,14 +257,23 @@
                 prod = ext * padded[8 * a : 8 * a + rows + 8]
                 result[o - 1] = jnp.sum(prod, axis=0, keepdims=True)
         result[KSIZE] = jnp.zeros((1, LANES), F32)
-        out_ref[: KSIZE + 1, lanes] = jnp.concatenate(result, axis=0).astype(BF)
-        head = gm[:PAD]
-        tail = gm[rows - PAD :]
-        out_ref[KSIZE + 1 : KSIZE + 1 + PAD, lanes] = jnp.where(odd, head, tail).astype(BF)
-        out_ref[KSIZE + 1 + PAD :, lanes] = jnp.where(odd, tail, head).astype(BF)
+        return jnp.concatenate(result, axis=0)
+
+    def step(c, _):
+        keep_ref[:, chunk(c)] = terms(chunk(c + half_ref[0] * count))
+        give_ref[: KSIZE + 1, chunk(c)] = terms(chunk(c + (1 - half_ref[0]) * count)).astype(BF)
+        for n in range(2):
+            lanes = chunk(c + n * count)
+            head = gm_ref[:PAD, lanes]
+            tail = gm_ref[rows - PAD :, lanes]
+            at = n * PAD
+            give_ref[KSIZE + 1 + at : KSIZE + 1 + at + PAD, chunk(c)] = jnp.where(
+                odd, head, tail
+            ).astype(BF)
+            edge_ref[at : at + PAD, chunk(c)] = jnp.where(odd, tail, head).astype(BF)
         return 0
 
-    lax.fori_loop(0, width // LANES, step, 0)
+    lax.fori_loop(0, count, step, 0)
 
 
 def own_kernel(len_ref, first_ref, in_ref, gm_ref, taps_ref, attn_ref, own_ref):
@@ -266,28 +294,29 @@
 
 
 def final_kernel(
-    len_ref, first_ref, own_ref, near_ref, far_ref, taps_ref, mine_ref, gi_ref, gk_ref,
-    *, frames,
+    len_ref, first_ref, own_ref, near_ref, far_ref, taps_ref, gi_ref, *, frames,
 ):
     rows, width = own_ref.shape
     first = first_ref[0]
     live = live_rows(first, rows, len_ref[0])
-    near_edge = near_ref.at[KSIZE + 1 : KSIZE + 1 + PAD]
-    far_edge = far_ref.at[KSIZE + 1 :]
+    count = width // 2 // LANES
 
     def step(c, _):
-        lanes = chunk(c)
-        low, high = ends(first, near_edge, far_edge, lanes, rows, frames)
-        top, end = edge_convs(low, high, taps_ref, lanes, True)
-        gi_ref[:PAD, lanes] = (own_ref[:PAD, lanes] + live[:PAD] * top).astype(BF)
-        gi_ref[PAD : rows - PAD, lanes] = own_ref[PAD : rows - PAD, lanes].astype(BF)
-        gi_ref[rows - PAD :, lanes] = (
-            own_ref[rows - PAD :, lanes] + live[rows - PAD :] * end
-        ).astype(BF)
-        gk_ref[:, lanes] = mine_ref[:KSIZE, lanes].astype(F32) + far_ref[:KSIZE, lanes].astype(F32)
+        for n in range(2):
+            lanes = chunk(c + n * count)
+            at = KSIZE + 1 + n * PAD
+            low, high = ends(
+                first, near_ref.at[at : at + PAD], far_ref.at[at : at + PAD], chunk(c), rows, frames
+            )
+            top, end = edge_convs(low, high, taps_ref, lanes, True)
+            gi_ref[:PAD, lanes] = (own_ref[:PAD, lanes] + live[:PAD] * top).astype(BF)
+            gi_ref[PAD : rows - PAD, lanes] = own_ref[PAD : rows - PAD, lanes].astype(BF)
+            gi_ref[rows - PAD :, lanes] = (
+                own_ref[rows - PAD :, lanes] + live[rows - PAD :] * end
+            ).astype(BF)
         return 0
 
-    lax.fori_loop(0, width // LANES, step, 0)
+    lax.fori_loop(0, count, step, 0)
 
 
 def params(mib):
@@ -360,9 +389,9 @@
         cost_estimate=cost(3),
     )(lengths, first, own, x_near, x_far, kernel, gain, weights, douts)
 
-    block, step = 512, 1024
+    block, sstep, step = 512, 1024, 512
     heads_out = pl.pallas_call(
-        functools.partial(attn_kernel, block=block, step=step),
+        functools.partial(attn_kernel, block=block, sstep=sstep, step=step),
         name="attn",
         out_shape=sds((HEADS, 4 * HDIM, rows), BF),
         in_specs=[SMEM, VMEM],
@@ -372,8 +401,8 @@
             pltpu.VMEM((HDIM, frames), BF),
             pltpu.VMEM((2 * HDIM, frames), BF),
             pltpu.VMEM((frames, 2 * HDIM), BF),
-            pltpu.VMEM((frames, block), F32),
-            pltpu.VMEM((frames, block), BF),
+            pltpu.VMEM((2, frames, block), F32),
+            pltpu.VMEM((2, frames, block), BF),
             pltpu.VMEM((frames, 2 * HDIM), F32),
         ],
         compiler_params=params(32),
@@ -390,23 +419,27 @@
         compiler_params=params(16),
         cost_estimate=cost(4),
     )(grads, q_weight, k_weight, v_weight, mixed, rstd, gain)
-    taps = pl.pallas_call(
+    here, gm = lax.optimization_barrier((here, gm))
+    half = ((here ^ (here >> 1)) & 1).astype(jnp.int32)
+    keep, give, edge = pl.pallas_call(
         taps_kernel,
         name="taps",
-        out_shape=sds((KSIZE + 1 + 2 * PAD, width), BF),
-        in_specs=[SMEM, SMEM] + [VMEM] * 4,
-        out_specs=VMEM,
+        out_shape=(
+            sds((KSIZE + 1, width // 2), F32),
+            sds((KSIZE + 1 + 2 * PAD, width // 2), BF),
+            sds((2 * PAD, width // 2), BF),
+        ),
+        in_specs=[SMEM] * 3 + [VMEM] * 4,
+        out_specs=(VMEM,) * 3,
         compiler_params=params(16),
         cost_estimate=cost(3),
-    )(lengths, first, inputs, x_near, x_far, gm)
-
-    got = near(taps[: KSIZE + 1 + PAD])
-    total = taps[: KSIZE + 1].astype(F32) + got[: KSIZE + 1].astype(F32)
-    for bit in (4, 8):
-        mine = total.astype(BF)
-        total = mine.astype(F32) + peer(mine, lambda i: i ^ bit).astype(F32)
-    mine = jnp.concatenate([total.astype(BF), taps[KSIZE + 1 + PAD :]], axis=0)
-    last = far(mine)
+    )(lengths, first, half.reshape(1), inputs, x_near, x_far, gm)
+
+    got = near(give)
+    mine = (keep + got[: KSIZE + 1].astype(F32)).astype(BF)
+    one, two, three = (peer(mine, lambda i: i ^ bits).astype(F32) for bits in (4, 8, 12))
+    mine = ((mine.astype(F32) + one) + (two + three)).astype(BF)
+    last = far(jnp.concatenate([mine, edge], axis=0))
     attn, own_gi = pl.pallas_call(
         own_kernel,
         name="own",
@@ -416,15 +449,20 @@
         compiler_params=params(16),
         cost_estimate=cost(3),
     )(lengths, first, grads, gm, kernel)
-    grad_input, grad_kernel = pl.pallas_call(
+    mine = (mine.astype(F32) + last[: KSIZE + 1].astype(F32)).astype(BF)
+    other = near(mine)
+    grad_input = pl.pallas_call(
         functools.partial(final_kernel, frames=frames),
         name="final",
-        out_shape=(sds((rows, width), BF), sds((KSIZE, width), F32)),
-        in_specs=[SMEM, SMEM] + [VMEM] * 5,
-        out_specs=(VMEM,) * 2,
+        out_shape=sds((rows, width), BF),
+        in_specs=[SMEM, SMEM] + [VMEM] * 4,
+        out_specs=VMEM,
         compiler_params=params(16),
         cost_estimate=cost(1),
-    )(lengths, first, own_gi, got, last, kernel, mine)
+    )(lengths, first, own_gi, got, last, kernel)
+    left = jnp.where(half == 0, mine, other)
+    right = jnp.where(half == 0, other, mine)
+    grad_kernel = jnp.concatenate([left, right], axis=1)[:KSIZE].astype(F32)
     return (attn, grad_input, grad_kernel)
 
 

time: 136 us -> 131 us (0.963)
  the two profiles are of different devices: /device:TPU:34 before, /device:TPU:71 now
where the time goes in v3:
time: 131 us; the launch traced here: 129 us
  blocking collectives  69.2 us (53%)
  Pallas kernels  31.6 us (24%)
  starting transfers between devices  17.2 us (13%)
  waiting for transfers between devices  7.52 us (6%)
  between operations  1.43 us (1%)
    all_to_all x1, blocking collectives, local(): a2a(send)  36.3 us
    all_to_all x1, blocking collectives, local(): grads = a2a(heads_out)  32.9 us
    ppermute x8, starting transfers between devices, peer(): return lax.ppermute(mine, 'seq', [(i, move(i)) for i in range(count)])  17.2 us
    pallas_call x1, Pallas kernels, local(): pl.pallas_call(functools.partial(attn_kernel, block=block, sstep=sstep, s...  14.5 us
    ppermute x8, waiting for transfers between devices, peer(): return lax.ppermute(mine, 'seq', [(i, move(i)) for i in range(count)])  7.52 us
    pallas_call x1, Pallas kernels, local(): pl.pallas_call(early_kernel, name='early', out_shape=(pltpu.VMEM((rows, w...  4.14 us
    pallas_call x1, Pallas kernels, local(): pl.pallas_call(back_kernel, name='back', out_shape=sds((rows, width), F32...  3.41 us
    pallas_call x1, Pallas kernels, local(): pl.pallas_call(own_kernel, name='own', out_shape=(sds((rows, feats), BF),...  3.09 us
  transfers between devices with their start and end apart: 8, of which 5 were waited for; matrix products, arithmetic and copies ran while one was open for 0% of the time, Pallas kernels for 7%

profile of v3, /device:TPU:71, one launch (start us, length us, event | category | flops | bytes accessed | tf_op | source)
XLA Modules:
  0.0 128.6 jit_solution(10736957405416654369)
XLA Ops:
  0.6 0.8 constant_dynamic-slice_fusion
  1.5 5.7 %collective-permute-start.1 = (bf16[16,1536]{1,0:T(8,128)(2,1)S(1)}, bf16[16,1536]{1,0:T(8,128)(2,1)S(1)}, u32[]{:S(2)}, u32[]{:S(2)}) collective-permute-start(bf16[16,1536]{1,0:T(8,128)(2,1)S(1)} %get-tuple-element.29), channel_id=1, source_target_pairs={{0,240},{16,32},{32,16},{48,64},{64,48},{80,96},{96,80},{112,128},... | collective-permute-start | bytes 147464 | tf_op jit(solution)/shard_map/ppermute | solution.py:342
  7.2 2.3 %collective-permute-start = (bf16[16,1536]{1,0:T(8,128)(2,1)S(1)}, bf16[16,1536]{1,0:T(8,128)(2,1)S(1)}, u32[]{:S(2)}, u32[]{:S(2)}) collective-permute-start(bf16[16,1536]{1,0:T(8,128)(2,1)S(1)} %get-tuple-element.30), channel_id=1, source_target_pairs={{0,16},{16,0},{32,48},{48,32},{64,80},{80,64},{96,112},{112,96},{1... | collective-permute-start | bytes 147464 | tf_op jit(solution)/shard_map/ppermute | solution.py:342
  10.2 4.1 %early.1 = (f32[128,1536]{1,0:T(8,128)S(1)}, bf16[3,1536,1024]{2,1,0:T(8,128)(2,1)S(1)}, bf16[16,64,128]{2,1,0:T(8,128)(2,1)S(1)}) custom-call(s32[1]{0:T(128)S(6)} %copy.11.len_ref, s32[1]{0:T(128)} %bitcast.first_ref, bf16[128,1536]{1,0:T(8,128)(2,1)} %x_ref.1, f32[31,1536]{1,0:T(8,128)} %taps_ref.5, bf16[128,1024]{1,0:T(8,128)(2,1)} %g_hbm.1, ...), custom_call_target="tpu_custom_call" | custom-call | flops 6600000000 | bytes 1024 | tf_op jit(solution)/shard_map/early/pallas_call | solution.py:359
  14.4 2.4 %pre.1 = (bf16[16,256,128]{2,1,0:T(8,128)(2,1)S(1)}, f32[128,1536]{1,0:T(8,128)S(1)}, f32[128,128]{1,0:T(8,128)S(1)}) custom-call(s32[1]{0:T(128)S(6)} %copy.11.len_ref, s32[1]{0:T(128)} %bitcast.first_ref, f32[128,1536]{1,0:T(8,128)S(1)} %get-tuple-element.16.conv_ref, bf16[16,1536]{1,0:T(8,128)(2,1)S(1)} %collective-permute-done.near_ref, ...), custom_call_target="tpu_custom_call" | custom-call | flops 3300000000 | bytes 1024 | tf_op jit(solution)/shard_map/pre/pallas_call | solution.py:378
  16.8 36.3 %all_to_all.10.in_ref = bf16[16,256,128]{2,1,0:T(8,128)(2,1)S(1)} all-to-all(bf16[16,256,128]{2,1,0:T(8,128)(2,1)S(1)} %get-tuple-element.19), channel_id=1, replica_groups=mesh['seq'=16,'dp'=16] {'seq'}, dimensions={0} | all-to-all | bytes 2097152 | tf_op jit(solution)/shard_map/all_to_all | solution.py:410
  53.1 14.5 %attn.1 = bf16[16,256,128]{2,1,0:T(8,128)(2,1)S(1)} custom-call(s32[1]{0:T(128)S(6)} %copy.11.len_ref, bf16[16,256,128]{2,1,0:T(8,128)(2,1)S(1)} %all_to_all.10.in_ref), custom_call_target="tpu_custom_call" | custom-call | flops 18699999232 | bytes 1024 | tf_op jit(solution)/shard_map/attn/pallas_call | solution.py:393
  67.6 32.9 %all_to_all.11.in_ref = bf16[16,256,128]{2,1,0:T(8,128)(2,1)S(1)} all-to-all(bf16[16,256,128]{2,1,0:T(8,128)(2,1)S(1)} %attn.1), channel_id=1, replica_groups=mesh['seq'=16,'dp'=16] {'seq'}, dimensions={0} | all-to-all | bytes 2097152 | tf_op jit(solution)/shard_map/all_to_all | solution.py:411
  100.6 3.4 %back.1.gm_ref = f32[128,1536]{1,0:T(8,128)S(1)} custom-call(bf16[16,256,128]{2,1,0:T(8,128)(2,1)S(1)} %all_to_all.11.in_ref, bf16[1536,1024]{1,0:T(8,128)(2,1)S(1)} %copy-done.1, bf16[1536,1024]{1,0:T(8,128)(2,1)S(1)} %copy-done.2, bf16[1536,1024]{1,0:T(8,128)(2,1)S(1)} %copy-done.3, f32[128,1536]{1,0:T(8,128)S(1)} %get-tuple-element.20.mixed_ref, ...), custom_call_target="tpu_custom_call" | custom-call | flops 4400000000 | bytes 1024 | tf_op jit(solution)/shard_map/back/pallas_call | solution.py:413
  104.0 2.6 %taps.1 = (f32[32,768]{1,0:T(8,128)S(1)}, bf16[64,768]{1,0:T(8,128)(2,1)S(1)}, bf16[32,768]{1,0:T(8,128)(2,1)S(1)}) custom-call(s32[1]{0:T(128)S(6)} %copy.11.len_ref, s32[1]{0:T(128)} %bitcast.first_ref, s32[1]{0:T(128)} %bitcast.1.half_ref, bf16[128,1536]{1,0:T(8,128)(2,1)S(1)} %copy-done, bf16[16,1536]{1,0:T(8,128)(2,1)S(1)} %collective-permute-done.near_ref, ...), custom_call_target="tpu_custom_call" | custom-call | flops 3300000000 | bytes 1024 | tf_op jit(solution)/shard_map/taps/pallas_call | solution.py:424
  106.6 0.5 collective-permute-start.2
  107.2 0.9 collective-permute-done.2.near_ref
  108.1 0.7 collective-permute-start.5
  108.8 0.3 collective-permute-start.4
  109.1 2.4 %collective-permute-start.3 = (bf16[32,768]{1,0:T(8,128)(2,1)S(1)}, bf16[32,768]{1,0:T(8,128)(2,1)S(1)}, u32[]{:S(2)}, u32[]{:S(2)}) collective-permute-start(bf16[32,768]{1,0:T(8,128)(2,1)S(1)} %add_convert_fusion.2), channel_id=1, source_target_pairs={{0,64},{16,80},{32,96},{48,112},{64,0},{80,16},{96,32},{112,48},{1... | collective-permute-start | bytes 147464 | tf_op jit(solution)/shard_map/ppermute | solution.py:342
  111.5 0.9 collective-permute-done.5
  112.4 1.0 collective-permute-done.4
  113.3 0.4 collective-permute-done.3
  113.8 1.3 %collective-permute-start.6 = (bf16[64,768]{1,0:T(8,128)(2,1)S(1)}, bf16[64,768]{1,0:T(8,128)(2,1)S(1)}, u32[]{:S(2)}, u32[]{:S(2)}) collective-permute-start(bf16[64,768]{1,0:T(8,128)(2,1)S(1)} %pad_maximum_fusion.1), channel_id=1, source_target_pairs={{0,240},{16,32},{32,16},{48,64},{64,48},{80,96},{96,80},{112,128},... | collective-permute-start | bytes 294920 | tf_op jit(solution)/shard_map/ppermute | solution.py:342
  115.1 3.1 %own.1 = (bf16[128,1024]{1,0:T(8,128)(2,1)}, f32[128,1536]{1,0:T(8,128)S(1)}) custom-call(s32[1]{0:T(128)S(6)} %copy.11.len_ref, s32[1]{0:T(128)} %bitcast.first_ref, bf16[16,256,128]{2,1,0:T(8,128)(2,1)S(1)} %all_to_all.11.in_ref, f32[128,1536]{1,0:T(8,128)S(1)} %back.1.gm_ref, f32[31,1536]{1,0:T(8,128)S(1)} %copy-done.4), custom_call_target="tpu_custom_call" | custom-call | flops 3300000000 | bytes 1024 | tf_op jit(solution)/shard_map/own/pallas_call | solution.py:443
  118.2 4.3 %collective-permute-done.6.far_ref = bf16[64,768]{1,0:T(8,128)(2,1)S(1)} collective-permute-done((bf16[64,768]{1,0:T(8,128)(2,1)S(1)}, bf16[64,768]{1,0:T(8,128)(2,1)S(1)}, u32[]{:S(2)}, u32[]{:S(2)}) %collective-permute-start.6) | collective-permute-done | bytes 98336 | tf_op jit(solution)/shard_map/ppermute | solution.py:342
  122.5 4.0 %collective-permute-start.7 = (bf16[32,768]{1,0:T(8,128)(2,1)S(1)}, bf16[32,768]{1,0:T(8,128)(2,1)S(1)}, u32[]{:S(2)}, u32[]{:S(2)}) collective-permute-start(bf16[32,768]{1,0:T(8,128)(2,1)S(1)} %add_convert_fusion), channel_id=1, source_target_pairs={{0,16},{16,0},{32,48},{48,32},{64,80},{80,64},{96,112},{112,96},{1... | collective-permute-start | bytes 147464 | tf_op jit(solution)/shard_map/ppermute | solution.py:342
  126.5 1.4 %final.1 = bf16[128,1536]{1,0:T(8,128)(2,1)} custom-call(s32[1]{0:T(128)S(6)} %copy.11.len_ref, s32[1]{0:T(128)} %bitcast.first_ref, f32[128,1536]{1,0:T(8,128)S(1)} %get-tuple-element.24.own_ref, bf16[64,768]{1,0:T(8,128)(2,1)S(1)} %collective-permute-done.2.near_ref, bf16[64,768]{1,0:T(8,128)(2,1)S(1)} %collective-permute-done.6.far_ref, ...), custom_call_target="tpu_custom_call" | custom-call | flops 1100000000 | bytes 1024 | tf_op jit(solution)/shard_map/final/pallas_call | solution.py:454
  127.9 0.7 fusion
  (21 shorter events, 0.1 us)
Async XLA Ops:
  1.5 12.9 %collective-permute-start.1 = (bf16[16,1536]{1,0:T(8,128)(2,1)S(1)}, bf16[16,1536]{1,0:T(8,128)(2,1)S(1)}, u32[]{:S(2)}, u32[]{:S(2)}) collective-permute-start(bf16[16,1536]{1,0:T(8,128)(2,1)S(1)} %get-tuple-element.29), channel_id=1, source_target_pairs={{0,240},{16,32},{32,16},{48,64},{64,48},{80,96},{96,80},{112,128},... | collective-permute-start | bytes 147464 | tf_op jit(solution)/shard_map/ppermute | solution.py:342
  7.2 7.1 %collective-permute-start = (bf16[16,1536]{1,0:T(8,128)(2,1)S(1)}, bf16[16,1536]{1,0:T(8,128)(2,1)S(1)}, u32[]{:S(2)}, u32[]{:S(2)}) collective-permute-start(bf16[16,1536]{1,0:T(8,128)(2,1)S(1)} %get-tuple-element.30), channel_id=1, source_target_pairs={{0,16},{16,0},{32,48},{48,32},{64,80},{80,64},{96,112},{112,96},{1... | collective-permute-start | bytes 147464 | tf_op jit(solution)/shard_map/ppermute | solution.py:342
  10.2 4.2 %copy-start.5 = (f32[1536]{0:T(1024)S(1)}, f32[1536]{0:T(1024)}, u32[]{:S(2)}) copy-start(f32[1536]{0:T(1024)} %param.11) | copy-start | bytes 18436
  10.2 4.2 %copy-start.4 = (f32[31,1536]{1,0:T(8,128)S(1)}, f32[31,1536]{1,0:T(8,128)}, u32[]{:S(2)}) copy-start(f32[31,1536]{1,0:T(8,128)} %taps_ref.5) | copy-start | bytes 571396
  53.1 47.5 %copy-start.1 = (bf16[1536,1024]{1,0:T(8,128)(2,1)S(1)}, bf16[1536,1024]{1,0:T(8,128)(2,1)}, u32[]{:S(2)}) copy-start(bf16[1536,1024]{1,0:T(8,128)(2,1)} %wq_ref.3) | copy-start | bytes 9437188
  53.1 47.5 %copy-start.2 = (bf16[1536,1024]{1,0:T(8,128)(2,1)S(1)}, bf16[1536,1024]{1,0:T(8,128)(2,1)}, u32[]{:S(2)}) copy-start(bf16[1536,1024]{1,0:T(8,128)(2,1)} %wk_ref.3) | copy-start | bytes 9437188
  53.1 47.5 %copy-start.3 = (bf16[1536,1024]{1,0:T(8,128)(2,1)S(1)}, bf16[1536,1024]{1,0:T(8,128)(2,1)}, u32[]{:S(2)}) copy-start(bf16[1536,1024]{1,0:T(8,128)(2,1)} %wv_ref.3) | copy-start | bytes 9437188
  100.5 3.4 %copy-start = (bf16[128,1536]{1,0:T(8,128)(2,1)S(1)}, bf16[128,1536]{1,0:T(8,128)(2,1)}, u32[]{:S(2)}) copy-start(bf16[128,1536]{1,0:T(8,128)(2,1)} %x_ref.1) | copy-start | bytes 1179652
  106.6 1.5 %collective-permute-start.2 = (bf16[64,768]{1,0:T(8,128)(2,1)S(1)}, bf16[64,768]{1,0:T(8,128)(2,1)S(1)}, u32[]{:S(2)}, u32[]{:S(2)}) collective-permute-start(bf16[64,768]{1,0:T(8,128)(2,1)S(1)} %get-tuple-element.26), channel_id=1, source_target_pairs={{0,16},{16,0},{32,48},{48,32},{64,80},{80,64},{96,112},{112,96},{1... | collective-permute-start | bytes 294920 | tf_op jit(solution)/shard_map/ppermute | solution.py:342
  108.1 4.2 %collective-permute-start.5 = (bf16[32,768]{1,0:T(8,128)(2,1)S(1)}, bf16[32,768]{1,0:T(8,128)(2,1)S(1)}, u32[]{:S(2)}, u32[]{:S(2)}) collective-permute-start(bf16[32,768]{1,0:T(8,128)(2,1)S(1)} %add_convert_fusion.2), channel_id=1, source_target_pairs={{0,192},{16,208},{32,224},{48,240},{64,128},{80,144},{96,160},{112... | collective-permute-start | bytes 147464 | tf_op jit(solution)/shard_map/ppermute | solution.py:342
  108.8 4.6 %collective-permute-start.4 = (bf16[32,768]{1,0:T(8,128)(2,1)S(1)}, bf16[32,768]{1,0:T(8,128)(2,1)S(1)}, u32[]{:S(2)}, u32[]{:S(2)}) collective-permute-start(bf16[32,768]{1,0:T(8,128)(2,1)S(1)} %add_convert_fusion.2), channel_id=1, source_target_pairs={{0,128},{16,144},{32,160},{48,176},{64,192},{80,208},{96,224},{112... | collective-permute-start | bytes 147464 | tf_op jit(solution)/shard_map/ppermute | solution.py:342
  109.1 4.7 %collective-permute-start.3 = (bf16[32,768]{1,0:T(8,128)(2,1)S(1)}, bf16[32,768]{1,0:T(8,128)(2,1)S(1)}, u32[]{:S(2)}, u32[]{:S(2)}) collective-permute-start(bf16[32,768]{1,0:T(8,128)(2,1)S(1)} %add_convert_fusion.2), channel_id=1, source_target_pairs={{0,64},{16,80},{32,96},{48,112},{64,0},{80,16},{96,32},{112,48},{1... | collective-permute-start | bytes 147464 | tf_op jit(solution)/shard_map/ppermute | solution.py:342
  113.8 8.7 %collective-permute-start.6 = (bf16[64,768]{1,0:T(8,128)(2,1)S(1)}, bf16[64,768]{1,0:T(8,128)(2,1)S(1)}, u32[]{:S(2)}, u32[]{:S(2)}) collective-permute-start(bf16[64,768]{1,0:T(8,128)(2,1)S(1)} %pad_maximum_fusion.1), channel_id=1, source_target_pairs={{0,240},{16,32},{32,16},{48,64},{64,48},{80,96},{96,80},{112,128},... | collective-permute-start | bytes 294920 | tf_op jit(solution)/shard_map/ppermute | solution.py:342
  122.5 5.4 %collective-permute-start.7 = (bf16[32,768]{1,0:T(8,128)(2,1)S(1)}, bf16[32,768]{1,0:T(8,128)(2,1)S(1)}, u32[]{:S(2)}, u32[]{:S(2)}) collective-permute-start(bf16[32,768]{1,0:T(8,128)(2,1)S(1)} %add_convert_fusion), channel_id=1, source_target_pairs={{0,16},{16,0},{32,48},{48,32},{64,80},{80,64},{96,112},{112,96},{1... | collective-permute-start | bytes 147464 | tf_op jit(solution)/shard_map/ppermute | solution.py:342

commit v4 on v3

--- a/solution.py
+++ b/solution.py
@@ -18,6 +18,7 @@
 VMEM = pl.BlockSpec(memory_space=pltpu.VMEM)
 SMEM = pl.BlockSpec(memory_space=pltpu.SMEM)
 HBM = pl.BlockSpec(memory_space=pltpu.HBM)
+ANY = pl.BlockSpec(memory_space=pl.ANY)
 
 
 def live_rows(first, rows, length):
@@ -54,19 +55,24 @@
     return pl.ds(pl.multiple_of(c * LANES, LANES), LANES)
 
 
+def dout_kernel(len_ref, first_ref, g_ref, out_ref):
+    live = live_rows(first_ref[0], g_ref.shape[0], len_ref[0])
+    out_ref[...] = (g_ref[...].astype(F32) * live[:, 0:1]).T.astype(BF)
+
+
 def early_kernel(
-    len_ref, first_ref, x_hbm, taps_hbm, g_hbm, wq_ref, wk_ref, wv_ref,
-    conv_ref, w_ref, d_ref, x_ref, taps_ref, g_ref, sems,
+    len_ref, first_ref, x_hbm, taps_hbm, wq_ref, wk_ref, wv_ref,
+    conv_ref, w_ref, x_ref, taps_ref, sems,
 ):
     rows, width = x_ref.shape
-    moves = ((x_hbm, x_ref), (taps_hbm, taps_ref), (g_hbm, g_ref))
+    moves = ((x_hbm, x_ref), (taps_hbm, taps_ref))
     moves += tuple((w, w_ref.at[i]) for i, w in enumerate((wq_ref, wk_ref, wv_ref)))
     copies = [pltpu.make_async_copy(*m, sems.at[i]) for i, m in enumerate(moves)]
     for cp in copies:
         cp.start()
     live = live_rows(first_ref[0], rows, len_ref[0])
     zero = jnp.zeros((PAD, LANES), F32)
-    for cp in copies[:3]:
+    for cp in copies[:2]:
         cp.wait()
 
     def conv_step(c, _):
@@ -77,8 +83,7 @@
         return 0
 
     lax.fori_loop(0, width // LANES, conv_step, 0)
-    d_ref[...] = (g_ref[...].astype(F32) * live[:, 0:1]).T.astype(BF).reshape(d_ref.shape)
-    for cp in copies[3:]:
+    for cp in copies[2:]:
         cp.wait()
 
 
@@ -91,7 +96,7 @@
 
 def pre_kernel(
     len_ref, first_ref, conv_ref, near_ref, far_ref, taps_ref, gain_ref, w_ref, d_ref,
-    send_ref, mixed_ref, rstd_ref,
+    send_ref, all_ref, mixed_ref, rstd_ref,
 ):
     rows, width = conv_ref.shape
 
@@ -116,13 +121,15 @@
     normed = (mixed_ref[...] * rstd * gain_ref[...]).astype(BF)
     for i in range(3):
         heads = jnp.dot(normed, w_ref[i], preferred_element_type=F32)
-        send_ref[:, i * HDIM : (i + 1) * HDIM, :] = heads.T.astype(BF).reshape(HEADS, HDIM, rows)
-    send_ref[:, 3 * HDIM :, :] = d_ref[...]
+        heads = heads.T.astype(BF).reshape(HEADS, HDIM, rows)
+        send_ref[:, i * HDIM : (i + 1) * HDIM, :] = heads
+        all_ref[:, i * HDIM : (i + 1) * HDIM, :] = heads
+    all_ref[:, 3 * HDIM :, :] = d_ref[...]
 
 
 def attn_kernel(
-    len_ref, in_ref, out_ref, qt_scr, dt_scr, kvt_scr, kv_scr, s_scr, e_scr, acc_scr,
-    *, block, sstep, step,
+    len_ref, late_ref, part_hbm, whole_hbm, d_hbm, out_ref, in_ref, qt_scr, dt_scr, kvt_scr, kv_scr,
+    s_scr, e_scr, acc_scr, sems, *, block, sstep, step,
 ):
     count, _, rows = in_ref.shape
     frames = count * rows
@@ -132,6 +139,22 @@
     half = frames // 2
     steps = frames // step
     blocks = frames // block
+
+    @pl.when(late_ref[0] == 0)
+    def _():
+        cp = pltpu.make_async_copy(whole_hbm, in_ref, sems.at[0])
+        cp.start()
+        cp.wait()
+
+    @pl.when(late_ref[0] != 0)
+    def _():
+        first = pltpu.make_async_copy(part_hbm, in_ref.at[:, : 3 * HDIM], sems.at[0])
+        second = pltpu.make_async_copy(d_hbm, in_ref.at[:, 3 * HDIM :], sems.at[1])
+        first.start()
+        second.start()
+        first.wait()
+        second.wait()
+
     for s in range(count):
         at = slice(s * rows, (s + 1) * rows)
         qt_scr[:, at] = in_ref[s, 0:HDIM, :]
@@ -350,53 +373,77 @@
     a2a = functools.partial(
         lax.all_to_all, axis_name="seq", split_axis=0, concat_axis=0, tiled=True
     )
-    x_far = far(lax.dynamic_slice_in_dim(inputs, odd * (rows - PAD), PAD))
-    x_near = near(lax.dynamic_slice_in_dim(inputs, (1 - odd) * (rows - PAD), PAD))
+    slices = (
+        lax.dynamic_slice_in_dim(inputs, odd * (rows - PAD), PAD),
+        lax.dynamic_slice_in_dim(inputs, (1 - odd) * (rows - PAD), PAD),
+    )
+    for_far, for_near, after = lax.optimization_barrier(slices + (first,))
+    x_far = far(for_far)
+    x_near = near(for_near)
 
     def in_hbm(array):
         return pltpu.with_memory_space_constraint(array, pltpu.HBM)
 
-    own, weights, douts = pl.pallas_call(
+    late = lax.rem(lax.axis_index("dp"), 4) >= 2
+    douts = pl.pallas_call(
+        dout_kernel,
+        name="dout",
+        out_shape=sds((feats, rows), BF),
+        in_specs=[SMEM, SMEM, VMEM],
+        out_specs=VMEM,
+        compiler_params=params(4),
+        cost_estimate=cost(1),
+    )(lengths, after, in_hbm(grad_attn)).reshape(HEADS, HDIM, rows)
+    douts = lax.cond(late, a2a, lambda d: d, douts)
+    ready, douts = lax.optimization_barrier((first, douts))
+    own, weights = pl.pallas_call(
         early_kernel,
         name="early",
         out_shape=(
             pltpu.VMEM((rows, width), F32),
             pltpu.VMEM((3, width, feats), BF),
-            pltpu.VMEM((HEADS, HDIM, rows), BF),
         ),
-        in_specs=[SMEM, SMEM] + [HBM] * 6,
-        out_specs=(VMEM,) * 3,
+        in_specs=[SMEM, SMEM] + [HBM] * 5,
+        out_specs=(VMEM,) * 2,
         scratch_shapes=[
             pltpu.VMEM((rows, width), BF),
             pltpu.VMEM((KSIZE, width), F32),
-            pltpu.VMEM((rows, feats), BF),
-            pltpu.SemaphoreType.DMA((6,)),
+            pltpu.SemaphoreType.DMA((5,)),
         ],
         compiler_params=params(16),
         cost_estimate=cost(6),
-    )(lengths, first, *(in_hbm(a) for a in (inputs, kernel, grad_attn, q_weight, k_weight, v_weight)))
-    send, mixed, rstd = pl.pallas_call(
+    )(lengths, ready, *(in_hbm(a) for a in (inputs, kernel, q_weight, k_weight, v_weight)))
+    send, send_all, mixed, rstd = pl.pallas_call(
         pre_kernel,
         name="pre",
         out_shape=(
+            sds((HEADS, 3 * HDIM, rows), BF),
             sds((HEADS, 4 * HDIM, rows), BF),
             sds((rows, width), F32),
             sds((rows, LANES), F32),
         ),
         in_specs=[SMEM, SMEM] + [VMEM] * 7,
-        out_specs=(VMEM,) * 3,
+        out_specs=(VMEM,) * 4,
         compiler_params=params(16),
         cost_estimate=cost(3),
     )(lengths, first, own, x_near, x_far, kernel, gain, weights, douts)
 
     block, sstep, step = 512, 1024, 512
+
+    part, whole = lax.cond(
+        late,
+        lambda part, whole: lax.optimization_barrier((a2a(part), whole)),
+        lambda part, whole: (part, a2a(whole)),
+        send, send_all,
+    )
     heads_out = pl.pallas_call(
         functools.partial(attn_kernel, block=block, sstep=sstep, step=step),
         name="attn",
         out_shape=sds((HEADS, 4 * HDIM, rows), BF),
-        in_specs=[SMEM, VMEM],
+        in_specs=[SMEM, SMEM] + [ANY] * 3,
         out_specs=VMEM,
         scratch_shapes=[
+            pltpu.VMEM((HEADS, 4 * HDIM, rows), BF),
             pltpu.VMEM((HDIM, frames), BF),
             pltpu.VMEM((HDIM, frames), BF),
             pltpu.VMEM((2 * HDIM, frames), BF),
@@ -404,10 +451,11 @@
             pltpu.VMEM((2, frames, block), F32),
             pltpu.VMEM((2, frames, block), BF),
             pltpu.VMEM((frames, 2 * HDIM), F32),
+            pltpu.SemaphoreType.DMA((2,)),
         ],
         compiler_params=params(32),
-        cost_estimate=cost(17),
-    )(lengths, a2a(send))
+        cost_estimate=cost(15),
+    )(lengths, late.astype(jnp.int32).reshape(1), part, whole, douts)
     grads = a2a(heads_out)
 
     gm = pl.pallas_call(

time: 131 us -> 122 us (0.931); the launches traced: 129 us -> 121 us
  blocking collectives: 69.2 us -> 60.1 us
  Pallas kernels: 31.6 us -> 34.9 us
    all_to_all x1, blocking collectives: 32.9 us -> 22.8 us  [local(): grads = a2a(heads_out)]
    pallas_call x1 -> x2, Pallas kernels: 2.41 us -> 4.41 us  [the longest x1 3.32 us: local(): pl.pallas_call(pre_kernel, name='pre', out_shape=(sds((HEADS, 3 * HDIM, r...]
    pallas_call x1, Pallas kernels: 14.5 us -> 15.9 us  [local(): pl.pallas_call(functools.partial(attn_kernel, block=block, sstep=sstep, s...]
    all_to_all x1 -> x2, blocking collectives: 36.3 us -> 37.3 us  [the longest x1 20.9 us: local(): a2a(part)]
  transfers between devices with their start and end apart: 8 -> 8, of which waited for: 5 -> 5; matrix products, arithmetic and copies ran while one was open for 0% -> 0% of each run, Pallas kernels for 7% -> 8%
where the time goes in v4:
time: 122 us; the launch traced here: 121 us
  blocking collectives  60.1 us (49%)
  Pallas kernels  34.9 us (29%)
  starting transfers between devices  16.1 us (13%)
  waiting for transfers between devices  6.24 us (5%)
  local copies, waits for them, and re-layouts  2.02 us (2%)
  between operations  1.43 us (1%)
    all_to_all x1, blocking collectives, local(): grads = a2a(heads_out)  22.8 us
    all_to_all x1, blocking collectives, local(): a2a(part)  20.9 us
    all_to_all x1, blocking collectives, local(): douts = lax.cond(late, a2a, lambda d: d, douts)  16.4 us
    ppermute x8, starting transfers between devices, peer(): return lax.ppermute(mine, 'seq', [(i, move(i)) for i in range(count)])  16.1 us
    pallas_call x1, Pallas kernels, local(): pl.pallas_call(functools.partial(attn_kernel, block=block, sstep=sstep, s...  15.9 us
    ppermute x8, waiting for transfers between devices, peer(): return lax.ppermute(mine, 'seq', [(i, move(i)) for i in range(count)])  6.24 us
    pallas_call x1, Pallas kernels, local(): pl.pallas_call(early_kernel, name='early', out_shape=(pltpu.VMEM((rows, w...  4.05 us
    pallas_call x1, Pallas kernels, local(): pl.pallas_call(back_kernel, name='back', out_shape=sds((rows, width), F32...  3.41 us
  transfers between devices with their start and end apart: 8, of which 5 were waited for; matrix products, arithmetic and copies ran while one was open for 0% of the time, Pallas kernels for 8%

profile of v4, /device:TPU:71, one launch (start us, length us, event | category | flops | bytes accessed | tf_op | source)
XLA Modules:
  0.0 121.5 jit_solution(17451822956624295425)
XLA Ops:
  0.6 0.8 constant_dynamic-slice_fusion
  2.2 5.1 %collective-permute-start.1 = (bf16[16,1536]{1,0:T(8,128)(2,1)S(1)}, bf16[16,1536]{1,0:T(8,128)(2,1)S(1)}, u32[]{:S(2)}, u32[]{:S(2)}) collective-permute-start(bf16[16,1536]{1,0:T(8,128)(2,1)S(1)} %get-tuple-element.44), channel_id=1, source_target_pairs={{0,240},{16,32},{32,16},{48,64},{64,48},{80,96},{96,80},{112,128},... | collective-permute-start | bytes 147464 | tf_op jit(solution)/shard_map/ppermute | solution.py:365
  8.0 1.1 dout.1
  9.1 16.5 %conditional.2 = (bf16[16,64,128]{2,1,0:T(8,128)(2,1)S(1)}) conditional(s32[]{:T(128)} %convert_element_type.38, bf16[16,64,128]{2,1,0:T(8,128)(2,1)S(1)} %bitcast.4, bf16[16,64,128]{2,1,0:T(8,128)(2,1)S(1)} %bitcast.5), branch_computations={%region_0.0_spmd, %region_1.0_spmd} | conditional | bytes 1048584 | solution.py:397
  9.1 16.4 %all_to_all.17 = bf16[16,64,128]{2,1,0:T(8,128)(2,1)S(1)} all-to-all(bf16[16,64,128]{2,1,0:T(8,128)(2,1)S(1)} %copy.18), channel_id=1, replica_groups=mesh['seq'=16,'dp'=16] {'seq'}, dimensions={0} | all-to-all | bytes 524288 | tf_op jit(solution)/shard_map/cond/branch_1_fun/all_to_all | solution.py:397
  25.5 4.0 %early.1 = (f32[128,1536]{1,0:T(8,128)S(1)}, bf16[3,1536,1024]{2,1,0:T(8,128)(2,1)S(1)}) custom-call(s32[1]{0:T(128)S(6)} %copy.17.len_ref, s32[1]{0:T(128)} %bitcast.first_ref, bf16[128,1536]{1,0:T(8,128)(2,1)} %x_ref.1, f32[31,1536]{1,0:T(8,128)} %taps_ref.5, bf16[1536,1024]{1,0:T(8,128)(2,1)} %wq_ref.3, bf16[1536,1024]{1,0:T(8,128)(2,1)} %wk_ref.3, ...), custom_call_target="tpu_custom_call" | custom-call | flops 6600000000 | bytes 1024 | tf_op jit(solution)/shard_map/early/pallas_call | solution.py:399
  29.6 3.3 %pre.1 = (bf16[16,192,128]{2,1,0:T(8,128)(2,1)}, bf16[16,256,128]{2,1,0:T(8,128)(2,1)S(1)}, f32[128,1536]{1,0:T(8,128)S(1)}, f32[128,128]{1,0:T(8,128)S(1)}) custom-call(s32[1]{0:T(128)S(6)} %copy.17.len_ref, s32[1]{0:T(128)} %bitcast.first_ref, f32[128,1536]{1,0:T(8,128)S(1)} %get-tuple-element.42.conv_ref, ...), custom_call_target="tpu_custom_call" | custom-call | flops 3300000000 | bytes 1024 | tf_op jit(solution)/shard_map/pre/pallas_call | solution.py:416
  33.0 22.0 %conditional.3 = (bf16[16,192,128]{2,1,0:T(8,128)(2,1)}, bf16[16,256,128]{2,1,0:T(8,128)(2,1)S(1)}) conditional(s32[]{:T(128)} %convert_element_type.38, (bf16[16,256,128]{2,1,0:T(8,128)(2,1)S(1)}, bf16[16,192,128]{2,1,0:T(8,128)(2,1)}) %tuple.27, (bf16[16,192,128]{2,1,0:T(8,128)(2,1)}, bf16[16,256,128]{2,1,0:T(8,128)(2,1)S(1)}) %tuple.28), branch_computations={%region_2.0_spmd, %region_3.0_spmd} | conditional | bytes 4194320 | solution.py:433
  33.0 1.1 copy.20
  34.1 20.9 %all_to_all.19 = bf16[16,192,128]{2,1,0:T(8,128)(2,1)} all-to-all(bf16[16,192,128]{2,1,0:T(8,128)(2,1)S(1)} %copy.20), channel_id=1, replica_groups=mesh['seq'=16,'dp'=16] {'seq'}, dimensions={0} | all-to-all | bytes 1572864 | tf_op jit(solution)/shard_map/cond/branch_1_fun/all_to_all | solution.py:435
  55.0 15.9 %attn.1 = bf16[16,256,128]{2,1,0:T(8,128)(2,1)S(1)} custom-call(s32[1]{0:T(128)S(6)} %copy.17.len_ref, s32[1]{0:T(128)} %bitcast.1.late_ref, bf16[16,192,128]{2,1,0:T(8,128)(2,1)} %get-tuple-element.49.part_hbm, bf16[16,256,128]{2,1,0:T(8,128)(2,1)S(1)} %get-tuple-element.50.whole_hbm, bf16[16,64,128]{2,1,0:T(8,128)(2,1)S(1)} %get-tuple-element.68.d_ref.d_hbm), custom_call_target="tpu_custom_call" | custom-call | flops 16499999744 | bytes 1024 | tf_op jit(solution)/shard_map/attn/pallas_call | solution.py:439
  70.8 22.8 %all_to_all.20.in_ref = bf16[16,256,128]{2,1,0:T(8,128)(2,1)S(1)} all-to-all(bf16[16,256,128]{2,1,0:T(8,128)(2,1)S(1)} %attn.1), channel_id=1, replica_groups=mesh['seq'=16,'dp'=16] {'seq'}, dimensions={0} | all-to-all | bytes 2097152 | tf_op jit(solution)/shard_map/all_to_all | solution.py:459
  93.7 3.4 %back.1.gm_ref = f32[128,1536]{1,0:T(8,128)S(1)} custom-call(bf16[16,256,128]{2,1,0:T(8,128)(2,1)S(1)} %all_to_all.20.in_ref, bf16[1536,1024]{1,0:T(8,128)(2,1)S(1)} %copy-done.1, bf16[1536,1024]{1,0:T(8,128)(2,1)S(1)} %copy-done.2, bf16[1536,1024]{1,0:T(8,128)(2,1)S(1)} %copy-done.3, f32[128,1536]{1,0:T(8,128)S(1)} %get-tuple-element.51.mixed_ref, ...), custom_call_target="tpu_custom_call" | custom-call | flops 4400000000 | bytes 1024 | tf_op jit(solution)/shard_map/back/pallas_call | solution.py:461
  97.1 2.6 %taps.1 = (f32[32,768]{1,0:T(8,128)S(1)}, bf16[64,768]{1,0:T(8,128)(2,1)S(1)}, bf16[32,768]{1,0:T(8,128)(2,1)S(1)}) custom-call(s32[1]{0:T(128)S(6)} %copy.17.len_ref, s32[1]{0:T(128)} %bitcast.first_ref, s32[1]{0:T(128)} %bitcast.3.half_ref, bf16[128,1536]{1,0:T(8,128)(2,1)S(1)} %copy-done, bf16[16,1536]{1,0:T(8,128)(2,1)S(1)} %collective-permute-done.near_ref, ...), custom_call_target="tpu_custom_call" | custom-call | flops 3300000000 | bytes 1024 | tf_op jit(solution)/shard_map/taps/pallas_call | solution.py:472
  99.8 1.2 %collective-permute-start.2 = (bf16[64,768]{1,0:T(8,128)(2,1)S(1)}, bf16[64,768]{1,0:T(8,128)(2,1)S(1)}, u32[]{:S(2)}, u32[]{:S(2)}) collective-permute-start(bf16[64,768]{1,0:T(8,128)(2,1)S(1)} %get-tuple-element.57), channel_id=1, source_target_pairs={{0,16},{16,0},{32,48},{48,32},{64,80},{80,64},{96,112},{112,96},{1... | collective-permute-start | bytes 294920 | tf_op jit(solution)/shard_map/ppermute | solution.py:365
  101.0 0.9 collective-permute-done.2.near_ref
  102.8 2.5 %collective-permute-start.3 = (bf16[32,768]{1,0:T(8,128)(2,1)S(1)}, bf16[32,768]{1,0:T(8,128)(2,1)S(1)}, u32[]{:S(2)}, u32[]{:S(2)}) collective-permute-start(bf16[32,768]{1,0:T(8,128)(2,1)S(1)} %add_convert_fusion.2), channel_id=1, source_target_pairs={{0,64},{16,80},{32,96},{48,112},{64,0},{80,16},{96,32},{112,48},{1... | collective-permute-start | bytes 147464 | tf_op jit(solution)/shard_map/ppermute | solution.py:365
  105.3 0.9 collective-permute-done.5
  106.2 0.9 collective-permute-done.4
  107.7 1.9 %collective-permute-start.6 = (bf16[64,768]{1,0:T(8,128)(2,1)S(1)}, bf16[64,768]{1,0:T(8,128)(2,1)S(1)}, u32[]{:S(2)}, u32[]{:S(2)}) collective-permute-start(bf16[64,768]{1,0:T(8,128)(2,1)S(1)} %pad_maximum_fusion.1), channel_id=1, source_target_pairs={{0,240},{16,32},{32,16},{48,64},{64,48},{80,96},{96,80},{112,128},... | collective-permute-start | bytes 294920 | tf_op jit(solution)/shard_map/ppermute | solution.py:365
  109.6 3.1 %own.1 = (bf16[128,1024]{1,0:T(8,128)(2,1)}, f32[128,1536]{1,0:T(8,128)S(1)}) custom-call(s32[1]{0:T(128)S(6)} %copy.17.len_ref, s32[1]{0:T(128)} %bitcast.first_ref, bf16[16,256,128]{2,1,0:T(8,128)(2,1)S(1)} %all_to_all.20.in_ref, f32[128,1536]{1,0:T(8,128)S(1)} %back.1.gm_ref, f32[31,1536]{1,0:T(8,128)S(1)} %copy-done.4), custom_call_target="tpu_custom_call" | custom-call | flops 3300000000 | bytes 1024 | tf_op jit(solution)/shard_map/own/pallas_call | solution.py:491
  112.7 3.0 %collective-permute-done.6.far_ref = bf16[64,768]{1,0:T(8,128)(2,1)S(1)} collective-permute-done((bf16[64,768]{1,0:T(8,128)(2,1)S(1)}, bf16[64,768]{1,0:T(8,128)(2,1)S(1)}, u32[]{:S(2)}, u32[]{:S(2)}) %collective-permute-start.6) | collective-permute-done | bytes 98336 | tf_op jit(solution)/shard_map/ppermute | solution.py:365
  115.7 3.7 %collective-permute-start.7 = (bf16[32,768]{1,0:T(8,128)(2,1)S(1)}, bf16[32,768]{1,0:T(8,128)(2,1)S(1)}, u32[]{:S(2)}, u32[]{:S(2)}) collective-permute-start(bf16[32,768]{1,0:T(8,128)(2,1)S(1)} %add_convert_fusion), channel_id=1, source_target_pairs={{0,16},{16,0},{32,48},{48,32},{64,80},{80,64},{96,112},{112,96},{1... | collective-permute-start | bytes 147464 | tf_op jit(solution)/shard_map/ppermute | solution.py:365
  119.4 1.4 %final.1 = bf16[128,1536]{1,0:T(8,128)(2,1)} custom-call(s32[1]{0:T(128)S(6)} %copy.17.len_ref, s32[1]{0:T(128)} %bitcast.first_ref, f32[128,1536]{1,0:T(8,128)S(1)} %get-tuple-element.55.own_ref, bf16[64,768]{1,0:T(8,128)(2,1)S(1)} %collective-permute-done.2.near_ref, bf16[64,768]{1,0:T(8,128)(2,1)S(1)} %collective-permute-done.6.far_ref, ...), custom_call_target="tpu_custom_call" | custom-call | flops 1100000000 | bytes 1024 | tf_op jit(solution)/shard_map/final/pallas_call | solution.py:502
  (27 shorter events, 2.9 us)
Async XLA Ops:
  1.5 28.1 %collective-permute-start = (bf16[16,1536]{1,0:T(8,128)(2,1)S(1)}, bf16[16,1536]{1,0:T(8,128)(2,1)S(1)}, u32[]{:S(2)}, u32[]{:S(2)}) collective-permute-start(bf16[16,1536]{1,0:T(8,128)(2,1)S(1)} %get-tuple-element.43), channel_id=1, source_target_pairs={{0,16},{16,0},{32,48},{48,32},{64,80},{80,64},{96,112},{112,96},{1... | collective-permute-start | bytes 147464 | tf_op jit(solution)/shard_map/ppermute | solution.py:365
  2.2 27.4 %collective-permute-start.1 = (bf16[16,1536]{1,0:T(8,128)(2,1)S(1)}, bf16[16,1536]{1,0:T(8,128)(2,1)S(1)}, u32[]{:S(2)}, u32[]{:S(2)}) collective-permute-start(bf16[16,1536]{1,0:T(8,128)(2,1)S(1)} %get-tuple-element.44), channel_id=1, source_target_pairs={{0,240},{16,32},{32,16},{48,64},{64,48},{80,96},{96,80},{112,128},... | collective-permute-start | bytes 147464 | tf_op jit(solution)/shard_map/ppermute | solution.py:365
  25.5 4.1 %copy-start.5 = (f32[1536]{0:T(1024)S(1)}, f32[1536]{0:T(1024)}, u32[]{:S(2)}) copy-start(f32[1536]{0:T(1024)} %param.15) | copy-start | bytes 18436
  25.5 4.1 %copy-start.4 = (f32[31,1536]{1,0:T(8,128)S(1)}, f32[31,1536]{1,0:T(8,128)}, u32[]{:S(2)}) copy-start(f32[31,1536]{1,0:T(8,128)} %taps_ref.5) | copy-start | bytes 571396
  55.0 38.7 %copy-start.1 = (bf16[1536,1024]{1,0:T(8,128)(2,1)S(1)}, bf16[1536,1024]{1,0:T(8,128)(2,1)}, u32[]{:S(2)}) copy-start(bf16[1536,1024]{1,0:T(8,128)(2,1)} %wq_ref.3) | copy-start | bytes 9437188
  55.0 38.7 %copy-start.2 = (bf16[1536,1024]{1,0:T(8,128)(2,1)S(1)}, bf16[1536,1024]{1,0:T(8,128)(2,1)}, u32[]{:S(2)}) copy-start(bf16[1536,1024]{1,0:T(8,128)(2,1)} %wk_ref.3) | copy-start | bytes 9437188
  55.0 38.7 %copy-start.3 = (bf16[1536,1024]{1,0:T(8,128)(2,1)S(1)}, bf16[1536,1024]{1,0:T(8,128)(2,1)}, u32[]{:S(2)}) copy-start(bf16[1536,1024]{1,0:T(8,128)(2,1)} %wv_ref.3) | copy-start | bytes 9437188
  93.7 3.4 %copy-start = (bf16[128,1536]{1,0:T(8,128)(2,1)S(1)}, bf16[128,1536]{1,0:T(8,128)(2,1)}, u32[]{:S(2)}) copy-start(bf16[128,1536]{1,0:T(8,128)(2,1)} %x_ref.1) | copy-start | bytes 1179652
  99.8 2.2 %collective-permute-start.2 = (bf16[64,768]{1,0:T(8,128)(2,1)S(1)}, bf16[64,768]{1,0:T(8,128)(2,1)S(1)}, u32[]{:S(2)}, u32[]{:S(2)}) collective-permute-start(bf16[64,768]{1,0:T(8,128)(2,1)S(1)} %get-tuple-element.57), channel_id=1, source_target_pairs={{0,16},{16,0},{32,48},{48,32},{64,80},{80,64},{96,112},{112,96},{1... | collective-permute-start | bytes 294920 | tf_op jit(solution)/shard_map/ppermute | solution.py:365
  102.0 4.2 %collective-permute-start.5 = (bf16[32,768]{1,0:T(8,128)(2,1)S(1)}, bf16[32,768]{1,0:T(8,128)(2,1)S(1)}, u32[]{:S(2)}, u32[]{:S(2)}) collective-permute-start(bf16[32,768]{1,0:T(8,128)(2,1)S(1)} %add_convert_fusion.2), channel_id=1, source_target_pairs={{0,192},{16,208},{32,224},{48,240},{64,128},{80,144},{96,160},{112... | collective-permute-start | bytes 147464 | tf_op jit(solution)/shard_map/ppermute | solution.py:365
  102.6 4.6 %collective-permute-start.4 = (bf16[32,768]{1,0:T(8,128)(2,1)S(1)}, bf16[32,768]{1,0:T(8,128)(2,1)S(1)}, u32[]{:S(2)}, u32[]{:S(2)}) collective-permute-start(bf16[32,768]{1,0:T(8,128)(2,1)S(1)} %add_convert_fusion.2), channel_id=1, source_target_pairs={{0,128},{16,144},{32,160},{48,176},{64,192},{80,208},{96,224},{112... | collective-permute-start | bytes 147464 | tf_op jit(solution)/shard_map/ppermute | solution.py:365
  102.8 4.8 %collective-permute-start.3 = (bf16[32,768]{1,0:T(8,128)(2,1)S(1)}, bf16[32,768]{1,0:T(8,128)(2,1)S(1)}, u32[]{:S(2)}, u32[]{:S(2)}) collective-permute-start(bf16[32,768]{1,0:T(8,128)(2,1)S(1)} %add_convert_fusion.2), channel_id=1, source_target_pairs={{0,64},{16,80},{32,96},{48,112},{64,0},{80,16},{96,32},{112,48},{1... | collective-permute-start | bytes 147464 | tf_op jit(solution)/shard_map/ppermute | solution.py:365
  107.7 8.0 %collective-permute-start.6 = (bf16[64,768]{1,0:T(8,128)(2,1)S(1)}, bf16[64,768]{1,0:T(8,128)(2,1)S(1)}, u32[]{:S(2)}, u32[]{:S(2)}) collective-permute-start(bf16[64,768]{1,0:T(8,128)(2,1)S(1)} %pad_maximum_fusion.1), channel_id=1, source_target_pairs={{0,240},{16,32},{32,16},{48,64},{64,48},{80,96},{96,80},{112,128},... | collective-permute-start | bytes 294920 | tf_op jit(solution)/shard_map/ppermute | solution.py:365
  115.7 5.1 %collective-permute-start.7 = (bf16[32,768]{1,0:T(8,128)(2,1)S(1)}, bf16[32,768]{1,0:T(8,128)(2,1)S(1)}, u32[]{:S(2)}, u32[]{:S(2)}) collective-permute-start(bf16[32,768]{1,0:T(8,128)(2,1)S(1)} %add_convert_fusion), channel_id=1, source_target_pairs={{0,16},{16,0},{32,48},{48,32},{64,80},{80,64},{96,112},{112,96},{1... | collective-permute-start | bytes 147464 | tf_op jit(solution)/shard_map/ppermute | solution.py:365
